TPU v7x, 32 devices: a whole 2x2x4 slice. The times are simulated.
32 devices in a mesh: gx: 4 (over z), gy: 8 (over y, x, core).
Axes of the slice: x: 2, y: 2, z: 4, core: 2. Of those that a mesh axis runs over, the one named last changes fastest.
Arguments:
- scalars: float32 [4, 64, 64, 1024], P(None, None, 'gx', 'gy'), may hold values from -6 to 6
- winds: float32 [2, 64, 64, 1024], P(None, None, 'gx', 'gy'), may hold values from -0.6 to 0.6
- map_factor: float32 [64, 1024], P('gx', 'gy'), may hold values from 0.7 to 1.3
- urban_counts: int32 [32], P(('gx', 'gy')), may hold values from 64 to 256, as said below
- urban_cols: int32 [8192], P(('gx', 'gy')), may hold values from 0 to 2047, as said below
- street_class: int32 [8192], P(('gx', 'gy')), may hold values from 0 to 9
- area_table: float32 [10, 10], replicated, may hold values from 0.2 to 1
- wall_temp: float32 [10, 8192], P(None, ('gx', 'gy')), may hold values from -6 to 6
- indoor_temp: float32 [8192], P(('gx', 'gy')), may hold values from -6 to 6
Outputs:
- scalars_out: float32 [4, 64, 64, 1024], P(None, None, 'gx', 'gy')
- wall_out: float32 [10, 8192], P(None, ('gx', 'gy'))
- indoor_out: float32 [8192], P(('gx', 'gy'))
Inputs may be any that keep to these rules, and one draw needn't show every extreme that they name: `urban_counts`: some tile has exactly 256 live urban columns. `urban_cols`: the 256 entries of each tile are distinct cells of that tile, numbered x * 128 + y within it.
All inputs are finite; a program needn't handle non-finite values.
Results may differ from a plain program's by a relative error of at most 0.000056.
Values sent between devices are 32-bit elements; how exact they have to be, the bound alone decides.
No kernel may reach another device: no remote copies, remote signals or barrier semaphores. Data moves between devices by JAX's collectives and lax.ppermute only.
A program may use at most 192 MiB of HBM per device.

v0:
```python
import jax
import jax.numpy as jnp
from jax import lax
from jax.sharding import PartitionSpec as P

UL = 10
NWL = 10
NCLS = 10


heat_coef = 0.5
wall_coef = 0.05
conduct = 0.3
inner_coef = 0.2
room_coef = 0.1
flux_coef = 0.5


def padded(array, sides, width):
    for axis, dim in sides:
        size, length = (lax.axis_size(axis), array.shape[dim])
        up = [(i, (i + 1) % size) for i in range(size)]
        down = [(j, i) for i, j in up]
        last = lax.slice_in_dim(array, length - width, length, axis=dim)
        leading = lax.slice_in_dim(array, 0, width, axis=dim)
        before = lax.ppermute(last, axis, up)
        after = lax.ppermute(leading, axis, down)
        array = jnp.concatenate([before, array, after], axis=dim)
    return array


def trim_margin(array, have, want, axis):
    start = have - want
    length = array.shape[axis] - 2 * start
    return lax.slice_in_dim(array, start, start + length, axis=axis)


def face_divergence(field, speed, axis):
    length = field.shape[axis] - 5
    shifted = [lax.slice_in_dim(field, offset, offset + length, axis=axis) for offset in range(6)]
    face_speed = 0.5 * (
        lax.slice_in_dim(speed, 0, length, axis=axis - 1)
        + lax.slice_in_dim(speed, 1, length + 1, axis=axis - 1)
    )
    flux = (
        face_speed
        * (
            37.0 * (shifted[2] + shifted[3])
            - 8.0 * (shifted[1] + shifted[4])
            + (shifted[0] + shifted[5])
        )
        / 60.0
    )
    flux = (
        flux
        - jnp.abs(face_speed)
        * (
            shifted[5]
            - shifted[0]
            - 5.0 * (shifted[4] - shifted[1])
            + 10.0 * (shifted[3] - shifted[2])
        )
        / 60.0
    )
    return lax.slice_in_dim(flux, 1, length, axis=axis) - lax.slice_in_dim(
        flux, 0, length - 1, axis=axis
    )


def tendency(extended, margin, wind_ext, wind_margin, map_ext, map_margin):
    west_speed = trim_margin(
        trim_margin(wind_ext[0], wind_margin, margin - 2, 1), wind_margin, margin - 3, 2
    )
    south_speed = trim_margin(
        trim_margin(wind_ext[1], wind_margin, margin - 3, 1), wind_margin, margin - 2, 2
    )
    west_div = face_divergence(trim_margin(extended, margin, margin - 3, 3), west_speed, 2)
    south_div = face_divergence(trim_margin(extended, margin, margin - 3, 2), south_speed, 3)
    factor = trim_margin(trim_margin(map_ext, map_margin, margin - 3, 0), map_margin, margin - 3, 1)
    return -(factor * factor) * (west_div + south_div)


def physics(packed):
    air_temp = packed[:UL]
    areas = packed[UL : 2 * UL]
    walls = packed[2 * UL : 2 * UL + NWL]
    indoor = packed[2 * UL + NWL]
    heat = heat_coef * areas * (walls[0] - air_temp)
    first = walls[0] - wall_coef * jnp.sum(heat, axis=0) + conduct * (walls[1] - walls[0])
    middle = walls[1:-1] + conduct * (walls[:-2] - 2.0 * walls[1:-1] + walls[2:])
    last = walls[-1] + conduct * (walls[-2] - walls[-1]) + inner_coef * (indoor - walls[-1])
    indoor_new = indoor + room_coef * (walls[-1] - indoor)
    return jnp.concatenate([heat, first[None], middle, last[None], indoor_new[None]], axis=0)


def per_device(
    scalars,
    winds,
    map_factor,
    urban_counts,
    urban_cols,
    street_class,
    area_table,
    wall_temp,
    indoor_temp,
):
    wind_ext = padded(winds, (("gx", 2), ("gy", 3)), 1)

    def section_rate(field):
        extended = padded(field, (("gx", 2), ("gy", 3)), 3)
        return tendency(extended, 3, wind_ext, 1, map_factor, 0)

    section_one = scalars + section_rate(scalars) / 3.0
    section_two = scalars + section_rate(section_one) / 2.0
    advanced = scalars + section_rate(section_two)
    tile_x = scalars.shape[2]
    tile_y = scalars.shape[3]
    slots = urban_cols.shape[0]
    lower = advanced[0, :UL].reshape(UL, tile_x * tile_y)
    air_temp = lower[:, urban_cols]
    classes = jnp.arange(NCLS, dtype=jnp.int32)
    onehot = (street_class[None, :] == classes[:, None]).astype(jnp.float32)
    areas = jnp.dot(
        area_table.T, onehot, precision=lax.Precision.HIGHEST, preferred_element_type=jnp.float32
    )
    packed = jnp.concatenate([air_temp, areas, wall_temp, indoor_temp[None]], axis=0)
    result = physics(packed)
    live = jnp.arange(slots, dtype=jnp.int32) < urban_counts[0]
    heating = jnp.where(live[None, :], flux_coef * result[:UL], 0.0)
    lower = lower.at[:, urban_cols].add(heating).reshape(UL, tile_x, tile_y)
    scalars_out = advanced.at[0, :UL].set(lower)
    wall_out = jnp.where(live[None, :], result[UL : UL + NWL], wall_temp)
    indoor_out = jnp.where(live, result[UL + NWL], indoor_temp)
    return (scalars_out, wall_out, indoor_out)


def solution(mesh):
    in_specs = (
        P(None, None, "gx", "gy"),
        P(None, None, "gx", "gy"),
        P("gx", "gy"),
        P(("gx", "gy")),
        P(("gx", "gy")),
        P(("gx", "gy")),
        P(),
        P(None, ("gx", "gy")),
        P(("gx", "gy")),
    )
    out_specs = (P(None, None, "gx", "gy"), P(None, ("gx", "gy")), P(("gx", "gy")))
    return jax.shard_map(
        per_device, mesh=mesh, in_specs=in_specs, out_specs=out_specs, check_vma=False
    )
```

profile of v0, /device:TPU:0, one launch (start us, length us, event | category | flops | bytes accessed | tf_op | source)
XLA Modules:
  0.0 213.4 jit_solution(15344696415934887934)
XLA Ops:
  2.0 5.1 %collective-permute-start.1 = (f32[2,64,1,128]{3,1,2,0:T(8,128)S(1)}, f32[2,64,1,128]{3,1,2,0:T(8,128)S(1)}, u32[]{:S(2)}, u32[]{:S(2)}) collective-permute-start(f32[2,64,1,128]{3,1,2,0:T(8,128)S(1)} %bitcast.22), channel_id=1, source_target_pairs={{8,0},{16,8},{24,16},{0,24},{9,1},{17,9},{25,17},{1,25},{10,2},{18... | collective-permute-start | bytes 196616 | tf_op jit(solution)/shard_map/ppermute | solution.py:27
  9.7 3.8 %collective-permute-start.5 = (f32[4,64,3,128]{3,1,2,0:T(8,128)}, f32[4,64,3,128]{3,1,2,0:T(8,128)}, u32[]{:S(2)}, u32[]{:S(2)}) collective-permute-start(f32[4,64,3,128]{3,1,2,0:T(8,128)} %copy.176), channel_id=1, source_target_pairs={{8,0},{16,8},{24,16},{0,24},{9,1},{17,9},{25,17},{1,25},{10,2},{18... | collective-permute-start | bytes 1179656 | tf_op jit(solution)/shard_map/ppermute | solution.py:27
  16.8 4.4 %copy.167 = f32[4,64,16,128]{1,2,3,0:T(8,128)} copy(f32[4,64,16,128]{3,2,1,0:T(8,128)} %param.11) | data formatting | bytes 4194304 | tf_op args[0]
  24.1 2.6 %copy.149 = f32[4,64,3,128]{1,2,3,0:T(4,128)} copy(f32[4,64,3,128]{3,1,2,0:T(8,128)} %collective-permute-done.5) | data formatting | bytes 786432 | tf_op jit(solution)/shard_map/ppermute | solution.py:27
  26.7 4.1 %collective-permute-done.4 = f32[4,64,3,128]{3,1,2,0:T(8,128)} collective-permute-done((f32[4,64,3,128]{3,1,2,0:T(8,128)}, f32[4,64,3,128]{3,1,2,0:T(8,128)}, u32[]{:S(2)}, u32[]{:S(2)}) %collective-permute-start.4) | collective-permute-done | bytes 393248 | tf_op jit(solution)/shard_map/ppermute | solution.py:26
  30.8 2.3 %copy.145 = f32[4,64,3,128]{1,2,3,0:T(4,128)} copy(f32[4,64,3,128]{3,1,2,0:T(8,128)} %collective-permute-done.4) | data formatting | bytes 786432 | tf_op jit(solution)/shard_map/ppermute | solution.py:26
  34.4 2.6 %collective-permute-start.7 = (f32[4,64,22,3]{1,2,3,0:T(8,128)S(1)}, f32[4,64,22,3]{1,2,3,0:T(8,128)S(1)}, u32[]{:S(2)}, u32[]{:S(2)}) collective-permute-start(f32[4,64,22,3]{1,2,3,0:T(8,128)S(1)} %get-tuple-element.42), channel_id=1, source_target_pairs={{1,0},{2,1},{3,2},{4,3},{5,4},{6,5},{7,6},{0,7},{9,8},{10,9},{11,1... | collective-permute-start | bytes 202760 | tf_op jit(solution)/shard_map/ppermute | solution.py:27
  37.0 8.8 %multiply_subtract_fusion.2 = f32[4,64,17,128]{1,2,3,0:T(8,128)} fusion(f32[4,64,16,128]{1,2,3,0:T(8,128)S(1)} %copy-done.1, f32[4,64,3,128]{1,2,3,0:T(4,128)S(1)} %copy-done.19, f32[4,64,3,128]{1,2,3,0:T(4,128)S(1)} %copy-done.16, f32[64,17,128]{0,1,2:T(8,128)S(1)} %get-tuple-element.27, f32[64,17,128]{0,1,2:T(8,128)S(1)} %get-tuple-element.28), kind=kLoop, calls=%fused_computation.52 | loop fusion | flops 13926400 | bytes 6225920 | tf_op jit(solution)/shard_map/sub | solution.py:55
  45.8 4.7 %maximum_maximum_fusion = (f32[4,64,22,131]{1,2,3,0:T(8,128)S(1)}, f32[4,64,22,131]{1,2,3,0:T(8,128)}) fusion(f32[4,64,3,128]{1,2,3,0:T(4,128)S(1)} %copy-done.16, f32[4,64,16,128]{1,2,3,0:T(8,128)S(1)} %copy-done.1, f32[4,64,3,128]{1,2,3,0:T(4,128)S(1)} %copy-done.19, f32[4,64,22,3]{1,2,3,0:T(8,128)S(1)} %collective-permute-done.6, ...), kind=kLoop, calls=%fused_computation.26 | loop fusion | flops 4426752 | bytes 8921088 | tf_op jit(solution)/shard_map/concatenate | solution.py:28
  50.5 11.0 %multiply_subtract_fusion.5 = f32[4,64,16,129]{1,2,3,0:T(8,128)} fusion(f32[4,64,22,131]{1,2,3,0:T(8,128)} %get-tuple-element.40, f32[4,64,22,131]{1,2,3,0:T(8,128)S(1)} %get-tuple-element.39, f32[64,16,129]{0,1,2:T(8,128)} %get-tuple-element.29, f32[64,16,129]{0,1,2:T(8,128)} %get-tuple-element.30), kind=kLoop, calls=%fused_computation.55 | loop fusion | flops 10039296 | bytes 15851520 | tf_op jit(solution)/shard_map/sub | solution.py:55
  61.4 7.3 %fusion.22 = f32[4,64,16,128]{1,2,3,0:T(8,128)S(1)} fusion(f32[4,64,16,128]{1,2,3,0:T(8,128)S(1)} %copy-done.1, f32[4,64,16,129]{1,2,3,0:T(8,128)} %multiply_subtract_fusion.5, f32[4,64,17,128]{1,2,3,0:T(8,128)} %multiply_subtract_fusion.2, f32[16,128]{0,1:T(8,128)S(1)} %copy.138), kind=kLoop, calls=%fused_computation.71 | loop fusion | flops 3145728 | bytes 12591104 | tf_op jit(solution)/shard_map/add | solution.py:113
  71.4 2.8 %collective-permute-start.9 = (f32[4,64,3,128]{3,1,2,0:T(8,128)S(1)}, f32[4,64,3,128]{3,1,2,0:T(8,128)S(1)}, u32[]{:S(2)}, u32[]{:S(2)}) collective-permute-start(f32[4,64,3,128]{3,1,2,0:T(8,128)S(1)} %copy.156), channel_id=1, source_target_pairs={{8,0},{16,8},{24,16},{0,24},{9,1},{17,9},{25,17},{1,25},{10,2},{18... | collective-permute-start | bytes 1179656 | tf_op jit(solution)/shard_map/ppermute | solution.py:27
  75.8 7.9 %collective-permute-done.9 = f32[4,64,3,128]{3,1,2,0:T(8,128)S(1)} collective-permute-done((f32[4,64,3,128]{3,1,2,0:T(8,128)S(1)}, f32[4,64,3,128]{3,1,2,0:T(8,128)S(1)}, u32[]{:S(2)}, u32[]{:S(2)}) %collective-permute-start.9) | collective-permute-done | bytes 393248 | tf_op jit(solution)/shard_map/ppermute | solution.py:27
  85.1 5.9 %collective-permute-done.8 = f32[4,64,3,128]{3,1,2,0:T(8,128)} collective-permute-done((f32[4,64,3,128]{3,1,2,0:T(8,128)}, f32[4,64,3,128]{3,1,2,0:T(8,128)}, u32[]{:S(2)}, u32[]{:S(2)}) %collective-permute-start.8) | collective-permute-done | bytes 393248 | tf_op jit(solution)/shard_map/ppermute | solution.py:26
  91.0 2.3 %copy.155 = f32[4,64,3,128]{1,2,3,0:T(4,128)} copy(f32[4,64,3,128]{3,1,2,0:T(8,128)} %collective-permute-done.8) | data formatting | bytes 786432 | tf_op jit(solution)/shard_map/ppermute | solution.py:26
  94.6 2.6 %collective-permute-start.11 = (f32[4,64,22,3]{1,2,3,0:T(8,128)S(1)}, f32[4,64,22,3]{1,2,3,0:T(8,128)S(1)}, u32[]{:S(2)}, u32[]{:S(2)}) collective-permute-start(f32[4,64,22,3]{1,2,3,0:T(8,128)S(1)} %get-tuple-element.38), channel_id=1, source_target_pairs={{1,0},{2,1},{3,2},{4,3},{5,4},{6,5},{7,6},{0,7},{9,8},{10,9},{11,1... | collective-permute-start | bytes 202760 | tf_op jit(solution)/shard_map/ppermute | solution.py:27
  97.2 11.2 %multiply_subtract_fusion.1 = f32[4,64,17,128]{1,2,3,0:T(8,128)} fusion(f32[4,64,16,128]{1,2,3,0:T(8,128)S(1)} %copy-done.7, f32[4,64,3,128]{1,2,3,0:T(4,128)} %copy.155, f32[4,64,3,128]{1,2,3,0:T(4,128)} %copy.157, f32[64,17,128]{0,1,2:T(8,128)S(1)} %copy-done.9, f32[64,17,128]{0,1,2:T(8,128)S(1)} %copy-done.12), kind=kLoop, calls=%fused_computation.51 | loop fusion | flops 13926400 | bytes 6225920 | tf_op jit(solution)/shard_map/sub | solution.py:55
  108.4 4.8 %maximum_maximum_fusion.1 = (f32[4,64,22,131]{1,2,3,0:T(8,128)S(1)}, f32[4,64,22,131]{1,2,3,0:T(8,128)}) fusion(f32[4,64,3,128]{1,2,3,0:T(4,128)S(1)} %copy-done.17, f32[4,64,16,128]{1,2,3,0:T(8,128)S(1)} %copy-done.7, f32[4,64,3,128]{1,2,3,0:T(4,128)S(1)} %copy-done.20, f32[4,64,22,3]{1,2,3,0:T(8,128)S(1)} %collective-permute-done.10, ...), kind=kLoop, calls=%fused_computation.28 | loop fusion | flops 4426752 | bytes 8921088 | tf_op jit(solution)/shard_map/concatenate | solution.py:28
  113.2 11.0 %multiply_subtract_fusion.4 = f32[4,64,16,129]{1,2,3,0:T(8,128)} fusion(f32[4,64,22,131]{1,2,3,0:T(8,128)} %get-tuple-element.36, f32[4,64,22,131]{1,2,3,0:T(8,128)S(1)} %get-tuple-element.35, f32[64,16,129]{0,1,2:T(8,128)} %get-tuple-element.29, f32[64,16,129]{0,1,2:T(8,128)} %get-tuple-element.30), kind=kLoop, calls=%fused_computation.54 | loop fusion | flops 10039296 | bytes 15851520 | tf_op jit(solution)/shard_map/sub | solution.py:55
  124.2 7.3 %fusion.18 = f32[4,64,16,128]{1,2,3,0:T(8,128)S(1)} fusion(f32[4,64,16,128]{1,2,3,0:T(8,128)S(1)} %copy-done.2, f32[4,64,16,129]{1,2,3,0:T(8,128)} %multiply_subtract_fusion.4, f32[4,64,17,128]{1,2,3,0:T(8,128)} %multiply_subtract_fusion.1, f32[16,128]{0,1:T(8,128)S(1)} %copy.138), kind=kLoop, calls=%fused_computation.65 | loop fusion | flops 3145728 | bytes 12591104 | tf_op jit(solution)/shard_map/add | solution.py:114
  134.1 3.1 %collective-permute-start.13 = (f32[4,64,3,128]{3,1,2,0:T(8,128)S(1)}, f32[4,64,3,128]{3,1,2,0:T(8,128)S(1)}, u32[]{:S(2)}, u32[]{:S(2)}) collective-permute-start(f32[4,64,3,128]{3,1,2,0:T(8,128)S(1)} %copy.163), channel_id=1, source_target_pairs={{8,0},{16,8},{24,16},{0,24},{9,1},{17,9},{25,17},{1,25},{10,2},{18... | collective-permute-start | bytes 1179656 | tf_op jit(solution)/shard_map/ppermute | solution.py:27
  138.2 8.6 %collective-permute-done.13 = f32[4,64,3,128]{3,1,2,0:T(8,128)S(1)} collective-permute-done((f32[4,64,3,128]{3,1,2,0:T(8,128)S(1)}, f32[4,64,3,128]{3,1,2,0:T(8,128)S(1)}, u32[]{:S(2)}, u32[]{:S(2)}) %collective-permute-start.13) | collective-permute-done | bytes 393248 | tf_op jit(solution)/shard_map/ppermute | solution.py:27
  148.1 6.6 %collective-permute-done.12 = f32[4,64,3,128]{3,1,2,0:T(8,128)} collective-permute-done((f32[4,64,3,128]{3,1,2,0:T(8,128)}, f32[4,64,3,128]{3,1,2,0:T(8,128)}, u32[]{:S(2)}, u32[]{:S(2)}) %collective-permute-start.12) | collective-permute-done | bytes 393248 | tf_op jit(solution)/shard_map/ppermute | solution.py:26
  154.7 2.3 %copy.162 = f32[4,64,3,128]{1,2,3,0:T(4,128)} copy(f32[4,64,3,128]{3,1,2,0:T(8,128)} %collective-permute-done.12) | data formatting | bytes 786432 | tf_op jit(solution)/shard_map/ppermute | solution.py:26
  158.3 2.6 %collective-permute-start.15 = (f32[4,64,22,3]{1,2,3,0:T(8,128)S(1)}, f32[4,64,22,3]{1,2,3,0:T(8,128)S(1)}, u32[]{:S(2)}, u32[]{:S(2)}) collective-permute-start(f32[4,64,22,3]{1,2,3,0:T(8,128)S(1)} %get-tuple-element.34), channel_id=1, source_target_pairs={{1,0},{2,1},{3,2},{4,3},{5,4},{6,5},{7,6},{0,7},{9,8},{10,9},{11,1... | collective-permute-start | bytes 202760 | tf_op jit(solution)/shard_map/ppermute | solution.py:27
  160.9 11.2 %multiply_subtract_fusion = f32[4,64,17,128]{1,2,3,0:T(8,128)} fusion(f32[4,64,16,128]{1,2,3,0:T(8,128)S(1)} %copy-done.5, f32[4,64,3,128]{1,2,3,0:T(4,128)} %copy.162, f32[4,64,3,128]{1,2,3,0:T(4,128)} %copy.164, f32[64,17,128]{0,1,2:T(8,128)S(1)} %copy-done.10, f32[64,17,128]{0,1,2:T(8,128)S(1)} %copy-done.13), kind=kLoop, calls=%fused_computation.50 | loop fusion | flops 13926400 | bytes 6225920 | tf_op jit(solution)/shard_map/sub | solution.py:55
  172.1 4.8 %maximum_maximum_fusion.2 = (f32[4,64,22,131]{1,2,3,0:T(8,128)S(1)}, f32[4,64,22,131]{1,2,3,0:T(8,128)}) fusion(f32[4,64,3,128]{1,2,3,0:T(4,128)S(1)} %copy-done.15, f32[4,64,16,128]{1,2,3,0:T(8,128)S(1)} %copy-done.5, f32[4,64,3,128]{1,2,3,0:T(4,128)S(1)} %copy-done.18, f32[4,64,22,3]{1,2,3,0:T(8,128)S(1)} %collective-permute-done.14, ...), kind=kLoop, calls=%fused_computation.30 | loop fusion | flops 4426752 | bytes 8921088 | tf_op jit(solution)/shard_map/concatenate | solution.py:28
  176.9 11.0 %multiply_subtract_fusion.3 = f32[4,64,16,129]{1,2,3,0:T(8,128)} fusion(f32[4,64,22,131]{1,2,3,0:T(8,128)} %get-tuple-element.32, f32[4,64,22,131]{1,2,3,0:T(8,128)S(1)} %get-tuple-element.31, f32[64,16,129]{0,1,2:T(8,128)} %get-tuple-element.29, f32[64,16,129]{0,1,2:T(8,128)} %get-tuple-element.30), kind=kLoop, calls=%fused_computation.53 | loop fusion | flops 10039296 | bytes 15851520 | tf_op jit(solution)/shard_map/sub | solution.py:55
  187.9 7.3 %fusion.14 = f32[4,64,16,128]{1,2,3,0:T(8,128)S(1)} fusion(f32[4,64,16,128]{1,2,3,0:T(8,128)S(1)} %copy-done.3, f32[4,64,16,129]{1,2,3,0:T(8,128)} %multiply_subtract_fusion.3, f32[4,64,17,128]{1,2,3,0:T(8,128)} %multiply_subtract_fusion, f32[16,128]{0,1:T(8,128)S(1)} %copy.138), kind=kLoop, calls=%fused_computation.59 | loop fusion | flops 2621440 | bytes 12591104 | tf_op jit(solution)/shard_map/add | solution.py:115
  198.8 2.3 %scatter_fusion = f32[10,2048]{0,1:T(8,128)S(1)} fusion(f32[10,2048]{0,1:T(8,128)S(1)} %bitcast.18, s32[256]{0:T(256)S(1)} %compare_select_fusion, f32[256,10]{1,0:T(8,128)S(1)} %copy.170), kind=kCustom, calls=%fused_computation.1 | custom fusion | flops 2560 | bytes 31744 | tf_op jit(solution)/shard_map/scatter-add | solution.py:130
  201.7 6.0 %scatter.4 = f32[4,64,16,128]{1,2,3,0:T(8,128)} dynamic-update-slice(f32[4,64,16,128]{1,2,3,0:T(8,128)} %copy-done.14, f32[1,10,16,128]{1,2,3,0:T(8,128)S(1)} %copy.171, s32[]{:T(128)} %constant.74.clone.1, s32[]{:T(128)} %constant.74.clone.1, s32[]{:T(128)} %constant.74.clone.1, s32[]{:T(128)} %constant.74.clone.1) | dynamic-update-slice | bytes 163844 | tf_op jit(solution)/shard_map/scatter | solution.py:131
  207.7 4.5 %copy.172 = f32[4,64,16,128]{3,2,1,0:T(8,128)} copy(f32[4,64,16,128]{1,2,3,0:T(8,128)} %scatter.4) | data formatting | bytes 4194304
  (116 shorter events, 29.0 us)
Async XLA Ops:
  0.6 197.8 %copy-start = (f32[10,10]{1,0:T(8,128)S(1)}, f32[10,10]{1,0:T(8,128)}, u32[]{:S(2)}) copy-start(f32[10,10]{1,0:T(8,128)} %param.17) | copy-start | bytes 1204
  0.6 13.7 %copy-start.21 = (f32[2,64,16,128]{3,2,1,0:T(8,128)S(1)}, f32[2,64,16,128]{3,2,1,0:T(8,128)}, u32[]{:S(2)}) copy-start(f32[2,64,16,128]{3,2,1,0:T(8,128)} %param.12) | copy-start | bytes 3145732
  2.0 13.4 %collective-permute-start.1 = (f32[2,64,1,128]{3,1,2,0:T(8,128)S(1)}, f32[2,64,1,128]{3,1,2,0:T(8,128)S(1)}, u32[]{:S(2)}, u32[]{:S(2)}) collective-permute-start(f32[2,64,1,128]{3,1,2,0:T(8,128)S(1)} %bitcast.22), channel_id=1, source_target_pairs={{8,0},{16,8},{24,16},{0,24},{9,1},{17,9},{25,17},{1,25},{10,2},{18... | collective-permute-start | bytes 196616 | tf_op jit(solution)/shard_map/ppermute | solution.py:27
  7.1 8.4 %collective-permute-start = (f32[2,64,1,128]{3,1,2,0:T(8,128)S(1)}, f32[2,64,1,128]{3,1,2,0:T(8,128)S(1)}, u32[]{:S(2)}, u32[]{:S(2)}) collective-permute-start(f32[2,64,1,128]{3,1,2,0:T(8,128)S(1)} %bitcast.21), channel_id=1, source_target_pairs={{0,8},{8,16},{16,24},{24,0},{1,9},{9,17},{17,25},{25,1},{2,10},{10... | collective-permute-start | bytes 196616 | tf_op jit(solution)/shard_map/ppermute | solution.py:26
  8.9 7.9 %copy-start.23 = (f32[16,128]{1,0:T(8,128)S(1)}, f32[16,128]{1,0:T(8,128)}, u32[]{:S(2)}) copy-start(f32[16,128]{1,0:T(8,128)} %param.13) | copy-start | bytes 24580
  9.7 14.4 %collective-permute-start.5 = (f32[4,64,3,128]{3,1,2,0:T(8,128)}, f32[4,64,3,128]{3,1,2,0:T(8,128)}, u32[]{:S(2)}, u32[]{:S(2)}) collective-permute-start(f32[4,64,3,128]{3,1,2,0:T(8,128)} %copy.176), channel_id=1, source_target_pairs={{8,0},{16,8},{24,16},{0,24},{9,1},{17,9},{25,17},{1,25},{10,2},{18... | collective-permute-start | bytes 1179656 | tf_op jit(solution)/shard_map/ppermute | solution.py:27
  14.3 16.5 %collective-permute-start.4 = (f32[4,64,3,128]{3,1,2,0:T(8,128)}, f32[4,64,3,128]{3,1,2,0:T(8,128)}, u32[]{:S(2)}, u32[]{:S(2)}) collective-permute-start(f32[4,64,3,128]{3,1,2,0:T(8,128)} %copy.175), channel_id=1, source_target_pairs={{0,8},{8,16},{16,24},{24,0},{1,9},{9,17},{17,25},{25,1},{2,10},{10... | collective-permute-start | bytes 1179656 | tf_op jit(solution)/shard_map/ppermute | solution.py:26
  15.7 5.7 %collective-permute-start.3 = (f32[2,64,18,1]{1,2,3,0:T(8,128)S(1)}, f32[2,64,18,1]{1,2,3,0:T(8,128)S(1)}, u32[]{:S(2)}, u32[]{:S(2)}) collective-permute-start(f32[2,64,18,1]{1,2,3,0:T(8,128)S(1)} %get-tuple-element.50), channel_id=1, source_target_pairs={{1,0},{2,1},{3,2},{4,3},{5,4},{6,5},{7,6},{0,7},{9,8},{10,9},{11,1... | collective-permute-start | bytes 27656 | tf_op jit(solution)/shard_map/ppermute | solution.py:27
  16.8 4.6 %collective-permute-start.2 = (f32[2,64,18,1]{1,2,3,0:T(8,128)S(1)}, f32[2,64,18,1]{1,2,3,0:T(8,128)S(1)}, u32[]{:S(2)}, u32[]{:S(2)}) collective-permute-start(f32[2,64,18,1]{1,2,3,0:T(8,128)S(1)} %get-tuple-element.49), channel_id=1, source_target_pairs={{0,1},{1,2},{2,3},{3,4},{4,5},{5,6},{6,7},{7,0},{8,9},{9,10},{10,1... | collective-permute-start | bytes 27656 | tf_op jit(solution)/shard_map/ppermute | solution.py:26
  24.1 12.9 %copy-start.8 = (f32[64,17,128]{0,1,2:T(8,128)}, f32[64,17,128]{0,1,2:T(8,128)S(1)}, u32[]{:S(2)}) copy-start(f32[64,17,128]{0,1,2:T(8,128)S(1)} %get-tuple-element.27) | copy-start | bytes 1671172
  24.1 12.9 %copy-start.11 = (f32[64,17,128]{0,1,2:T(8,128)}, f32[64,17,128]{0,1,2:T(8,128)S(1)}, u32[]{:S(2)}) copy-start(f32[64,17,128]{0,1,2:T(8,128)S(1)} %get-tuple-element.28) | copy-start | bytes 1671172
  34.3 11.5 %collective-permute-start.6 = (f32[4,64,22,3]{1,2,3,0:T(8,128)S(1)}, f32[4,64,22,3]{1,2,3,0:T(8,128)S(1)}, u32[]{:S(2)}, u32[]{:S(2)}) collective-permute-start(f32[4,64,22,3]{1,2,3,0:T(8,128)S(1)} %get-tuple-element.41), channel_id=1, source_target_pairs={{0,1},{1,2},{2,3},{3,4},{4,5},{5,6},{6,7},{7,0},{8,9},{9,10},{10,1... | collective-permute-start | bytes 202760 | tf_op jit(solution)/shard_map/ppermute | solution.py:26
  34.4 11.4 %collective-permute-start.7 = (f32[4,64,22,3]{1,2,3,0:T(8,128)S(1)}, f32[4,64,22,3]{1,2,3,0:T(8,128)S(1)}, u32[]{:S(2)}, u32[]{:S(2)}) collective-permute-start(f32[4,64,22,3]{1,2,3,0:T(8,128)S(1)} %get-tuple-element.42), channel_id=1, source_target_pairs={{1,0},{2,1},{3,2},{4,3},{5,4},{6,5},{7,6},{0,7},{9,8},{10,9},{11,1... | collective-permute-start | bytes 202760 | tf_op jit(solution)/shard_map/ppermute | solution.py:27
  71.4 12.4 %collective-permute-start.9 = (f32[4,64,3,128]{3,1,2,0:T(8,128)S(1)}, f32[4,64,3,128]{3,1,2,0:T(8,128)S(1)}, u32[]{:S(2)}, u32[]{:S(2)}) collective-permute-start(f32[4,64,3,128]{3,1,2,0:T(8,128)S(1)} %copy.156), channel_id=1, source_target_pairs={{8,0},{16,8},{24,16},{0,24},{9,1},{17,9},{25,17},{1,25},{10,2},{18... | collective-permute-start | bytes 1179656 | tf_op jit(solution)/shard_map/ppermute | solution.py:27
  75.1 15.9 %collective-permute-start.8 = (f32[4,64,3,128]{3,1,2,0:T(8,128)}, f32[4,64,3,128]{3,1,2,0:T(8,128)}, u32[]{:S(2)}, u32[]{:S(2)}) collective-permute-start(f32[4,64,3,128]{3,1,2,0:T(8,128)} %copy.154), channel_id=1, source_target_pairs={{0,8},{8,16},{16,24},{24,0},{1,9},{9,17},{17,25},{25,1},{2,10},{10... | collective-permute-start | bytes 1179656 | tf_op jit(solution)/shard_map/ppermute | solution.py:26
  85.1 12.2 %copy-start.9 = (f32[64,17,128]{0,1,2:T(8,128)S(1)}, f32[64,17,128]{0,1,2:T(8,128)}, u32[]{:S(2)}) copy-start(f32[64,17,128]{0,1,2:T(8,128)} %copy-done.8) | copy-start | bytes 1671172
  85.1 12.2 %copy-start.12 = (f32[64,17,128]{0,1,2:T(8,128)S(1)}, f32[64,17,128]{0,1,2:T(8,128)}, u32[]{:S(2)}) copy-start(f32[64,17,128]{0,1,2:T(8,128)} %copy-done.11) | copy-start | bytes 1671172
  94.5 13.9 %collective-permute-start.10 = (f32[4,64,22,3]{1,2,3,0:T(8,128)S(1)}, f32[4,64,22,3]{1,2,3,0:T(8,128)S(1)}, u32[]{:S(2)}, u32[]{:S(2)}) collective-permute-start(f32[4,64,22,3]{1,2,3,0:T(8,128)S(1)} %get-tuple-element.37), channel_id=1, source_target_pairs={{0,1},{1,2},{2,3},{3,4},{4,5},{5,6},{6,7},{7,0},{8,9},{9,10},{10,1... | collective-permute-start | bytes 202760 | tf_op jit(solution)/shard_map/ppermute | solution.py:26
  94.6 13.8 %copy-start.17 = (f32[4,64,3,128]{1,2,3,0:T(4,128)S(1)}, f32[4,64,3,128]{1,2,3,0:T(4,128)}, u32[]{:S(2)}) copy-start(f32[4,64,3,128]{1,2,3,0:T(4,128)} %copy.157) | copy-start | bytes 1179652
  94.6 13.8 %copy-start.20 = (f32[4,64,3,128]{1,2,3,0:T(4,128)S(1)}, f32[4,64,3,128]{1,2,3,0:T(4,128)}, u32[]{:S(2)}) copy-start(f32[4,64,3,128]{1,2,3,0:T(4,128)} %copy.155) | copy-start | bytes 1179652
  94.6 13.8 %collective-permute-start.11 = (f32[4,64,22,3]{1,2,3,0:T(8,128)S(1)}, f32[4,64,22,3]{1,2,3,0:T(8,128)S(1)}, u32[]{:S(2)}, u32[]{:S(2)}) collective-permute-start(f32[4,64,22,3]{1,2,3,0:T(8,128)S(1)} %get-tuple-element.38), channel_id=1, source_target_pairs={{1,0},{2,1},{3,2},{4,3},{5,4},{6,5},{7,6},{0,7},{9,8},{10,9},{11,1... | collective-permute-start | bytes 202760 | tf_op jit(solution)/shard_map/ppermute | solution.py:27
  113.2 11.0 %copy-start.2 = (f32[4,64,16,128]{1,2,3,0:T(8,128)S(1)}, f32[4,64,16,128]{1,2,3,0:T(8,128)}, u32[]{:S(2)}) copy-start(f32[4,64,16,128]{1,2,3,0:T(8,128)} %copy.167) | copy-start | bytes 6291460
  134.1 12.7 %collective-permute-start.13 = (f32[4,64,3,128]{3,1,2,0:T(8,128)S(1)}, f32[4,64,3,128]{3,1,2,0:T(8,128)S(1)}, u32[]{:S(2)}, u32[]{:S(2)}) collective-permute-start(f32[4,64,3,128]{3,1,2,0:T(8,128)S(1)} %copy.163), channel_id=1, source_target_pairs={{8,0},{16,8},{24,16},{0,24},{9,1},{17,9},{25,17},{1,25},{10,2},{18... | collective-permute-start | bytes 1179656 | tf_op jit(solution)/shard_map/ppermute | solution.py:27
  138.1 16.6 %collective-permute-start.12 = (f32[4,64,3,128]{3,1,2,0:T(8,128)}, f32[4,64,3,128]{3,1,2,0:T(8,128)}, u32[]{:S(2)}, u32[]{:S(2)}) collective-permute-start(f32[4,64,3,128]{3,1,2,0:T(8,128)} %copy.161), channel_id=1, source_target_pairs={{0,8},{8,16},{16,24},{24,0},{1,9},{9,17},{17,25},{25,1},{2,10},{10... | collective-permute-start | bytes 1179656 | tf_op jit(solution)/shard_map/ppermute | solution.py:26
  148.1 12.8 %copy-start.10 = (f32[64,17,128]{0,1,2:T(8,128)S(1)}, f32[64,17,128]{0,1,2:T(8,128)}, u32[]{:S(2)}) copy-start(f32[64,17,128]{0,1,2:T(8,128)} %copy-done.8) | copy-start | bytes 1671172
  148.1 12.8 %copy-start.13 = (f32[64,17,128]{0,1,2:T(8,128)S(1)}, f32[64,17,128]{0,1,2:T(8,128)}, u32[]{:S(2)}) copy-start(f32[64,17,128]{0,1,2:T(8,128)} %copy-done.11) | copy-start | bytes 1671172
  158.2 13.9 %collective-permute-start.14 = (f32[4,64,22,3]{1,2,3,0:T(8,128)S(1)}, f32[4,64,22,3]{1,2,3,0:T(8,128)S(1)}, u32[]{:S(2)}, u32[]{:S(2)}) collective-permute-start(f32[4,64,22,3]{1,2,3,0:T(8,128)S(1)} %get-tuple-element.33), channel_id=1, source_target_pairs={{0,1},{1,2},{2,3},{3,4},{4,5},{5,6},{6,7},{7,0},{8,9},{9,10},{10,1... | collective-permute-start | bytes 202760 | tf_op jit(solution)/shard_map/ppermute | solution.py:26
  158.3 13.8 %copy-start.15 = (f32[4,64,3,128]{1,2,3,0:T(4,128)S(1)}, f32[4,64,3,128]{1,2,3,0:T(4,128)}, u32[]{:S(2)}) copy-start(f32[4,64,3,128]{1,2,3,0:T(4,128)} %copy.164) | copy-start | bytes 1179652
  158.3 13.8 %copy-start.18 = (f32[4,64,3,128]{1,2,3,0:T(4,128)S(1)}, f32[4,64,3,128]{1,2,3,0:T(4,128)}, u32[]{:S(2)}) copy-start(f32[4,64,3,128]{1,2,3,0:T(4,128)} %copy.162) | copy-start | bytes 1179652
  158.3 13.8 %collective-permute-start.15 = (f32[4,64,22,3]{1,2,3,0:T(8,128)S(1)}, f32[4,64,22,3]{1,2,3,0:T(8,128)S(1)}, u32[]{:S(2)}, u32[]{:S(2)}) collective-permute-start(f32[4,64,22,3]{1,2,3,0:T(8,128)S(1)} %get-tuple-element.34), channel_id=1, source_target_pairs={{1,0},{2,1},{3,2},{4,3},{5,4},{6,5},{7,6},{0,7},{9,8},{10,9},{11,1... | collective-permute-start | bytes 202760 | tf_op jit(solution)/shard_map/ppermute | solution.py:27
  176.9 11.0 %copy-start.3 = (f32[4,64,16,128]{1,2,3,0:T(8,128)S(1)}, f32[4,64,16,128]{1,2,3,0:T(8,128)}, u32[]{:S(2)}) copy-start(f32[4,64,16,128]{1,2,3,0:T(8,128)} %copy.167) | copy-start | bytes 6291460
  201.7 10.5 %copy-start.25 = (f32[256]{0:T(256)S(1)}, f32[256]{0:T(256)}, u32[]{:S(2)}) copy-start(f32[256]{0:T(256)} %param.19) | copy-start | bytes 3076
  (12 other events, 37.7 us)
where the time goes:
time: 214 us; the launch traced here: 213 us
  other arithmetic  110 us (51%)
  local copies, waits for them, and re-layouts  44.7 us (21%)
  waiting for transfers between devices  33.1 us (15%)
  starting transfers between devices  23.9 us (11%)
    sub x6, other arithmetic, face_divergence(): flux - jnp.abs(face_speed) * (shifted[5] - shifted[0] - 5.0 * (shifted[4]...  64 us
    ppermute x8, starting transfers between devices, padded(): after = lax.ppermute(leading, axis, down)  23.7 us
    unnamed x59, local copies, waits for them, and re-layouts  17.7 us
    ppermute x8, waiting for transfers between devices, padded(): before = lax.ppermute(last, axis, up)  16.6 us
    ppermute x8, waiting for transfers between devices, padded(): after = lax.ppermute(leading, axis, down)  16.5 us
    concatenate x4, other arithmetic, padded(): array = jnp.concatenate([before, array, after], axis=dim)  14.9 us
    add x1, other arithmetic, per_device(): advanced = scalars + section_rate(section_two)  7.35 us
    add x1, other arithmetic, per_device(): section_one = scalars + section_rate(scalars) / 3.0  7.32 us
  transfers between devices with their start and end apart: 16, of which 5 were waited for; matrix products, arithmetic and copies ran while one was open for 24% of the time, Pallas kernels for 0%

commit v1 on v0

v1 whole, which is shorter than its diff:
```python
import functools

import jax
import jax.numpy as jnp
from jax import lax
from jax.experimental import pallas as pl
from jax.experimental.pallas import tpu as pltpu
from jax.sharding import PartitionSpec as P

UL = 10
NWL = 10
NCLS = 10
WIDTH = 3
GROUP = 8
CHUNKS = 2

heat_coef = 0.5
wall_coef = 0.05
conduct = 0.3
inner_coef = 0.2
room_coef = 0.1
flux_coef = 0.5
face_scale = 0.5 / 60.0


def lane_index(shape):
    return lax.broadcasted_iota(jnp.int32, shape, 1)


def rolled(array, shift):
    return pltpu.roll(array, shift % array.shape[1], 1)


def pack_edges(packed, row, x):
    moved = rolled(row, GROUP * x + WIDTH)
    lane = lane_index(row.shape)
    here = (lane >= GROUP * x) & (lane < GROUP * x + 2 * WIDTH)
    return moved if packed is None else jnp.where(here, moved, packed)


def ahead(row, halo, lane, k):
    if k > 0:
        return rolled(jnp.where(lane < k, halo, row), -k)
    return rolled(jnp.where(lane >= row.shape[1] + k, halo, row), -k)


def combine(a, b, c, d, e, f, speed):
    high = 37.0 * (c + d) - 8.0 * (b + e) + (a + f)
    damp = (f - a) - 5.0 * (e - b) + 10.0 * (d - c)
    return speed * high - jnp.abs(speed) * damp


def extract_kernel(tiles, x_size, with_wind, *refs):
    if with_wind:
        field, wind, low, high, packed = refs
    else:
        field, low, high, packed = refs
    rows = field.shape[0] // x_size

    def one(t, carry):
        base = pl.multiple_of(t * 8 * x_size, 8 * x_size)
        edges = None
        for x in range(x_size):
            row = field[pl.ds(base + x, 8, stride=x_size), :]
            if x < WIDTH:
                low[pl.ds(pl.multiple_of(x * rows + t * 8, 8), 8), :] = row
            if x >= x_size - WIDTH:
                at = (x - x_size + WIDTH) * rows
                high[pl.ds(pl.multiple_of(at + t * 8, 8), 8), :] = row
            edges = pack_edges(edges, row, x)
        packed[pl.ds(pl.multiple_of(t * 8, 8), 8), :] = edges
        return carry

    lax.fori_loop(0, rows // 8, one, 0)
    if with_wind:
        levels = wind.shape[0] // (2 * x_size)

        def one_wind(t, carry):
            base = pl.multiple_of(t * 8 * x_size, 8 * x_size)
            at = pl.ds(pl.multiple_of(WIDTH * rows + t * 8, 8), 8)
            low[at, :] = wind[pl.ds(base, 8, stride=x_size), :]
            high[at, :] = wind[pl.ds(base + x_size - 1, 8, stride=x_size), :]
            base = base + levels * x_size
            edges = None
            for x in range(x_size):
                edges = pack_edges(edges, wind[pl.ds(base + x, 8, stride=x_size), :], x)
            packed[pl.ds(pl.multiple_of(rows + t * 8, 8), 8), :] = edges
            return carry

        lax.fori_loop(0, levels // 8, one_wind, 0)


def wind_kernel(x_size, wind, west, east, south, north, own, speed_x, speed_y, speed_edge):
    levels = speed_x.shape[1]

    def one(t, carry):
        base = pl.multiple_of(t * 8 * x_size, 8 * x_size)
        at = pl.ds(pl.multiple_of(t * 8, 8), 8)
        before = west[at, :]
        for x in range(x_size + 1):
            now = east[at, :] if x == x_size else wind[pl.ds(base + x, 8, stride=x_size), :]
            speed_x[x, at, :] = face_scale * (before + now)
            before = now
        base = base + levels * x_size
        lane = lane_index(before.shape)
        first = (lane & (GROUP - 1)) < WIDTH
        halo = jnp.where(first, south[at, :], north[at, :])
        for x in range(x_size):
            row = wind[pl.ds(base + x, 8, stride=x_size), :]
            edge = rolled(halo, -(GROUP * x + WIDTH))
            speed_y[x, at, :] = face_scale * (row + ahead(row, edge, lane, 1))
        seam = jnp.where(first, south[at, :], own[at, :])
        speed_edge[at, :] = face_scale * (seam + rolled(seam, -1))
        return carry

    lax.fori_loop(0, levels // 8, one, 0)


def section_tile(t, x_size, divisor, load, base, halos, packs, speeds, factor, store):
    west, east = halos
    south, north, own = packs
    speed_x, speed_y, speed_edge = speeds
    at = pl.ds(pl.multiple_of(t * 8, 8), 8)
    south_edges = south[at, :]
    lane = lane_index(south_edges.shape)
    first = (lane & (GROUP - 1)) < WIDTH
    halo = jnp.where(first, south_edges, north[at, :])
    seam = jnp.where(first, south_edges, own[at, :])
    seam_flux = combine(*[rolled(seam, -k) for k in range(-2, 4)], speed_edge[at, :])

    def cell(x):
        if x < 0:
            return west[x + WIDTH][at, :]
        if x >= x_size:
            return east[x - x_size][at, :]
        return load(x, at)

    q = [cell(x) for x in range(-3, 2)]
    d1 = [q[i + 1] - q[i] for i in range(4)]
    d2 = [d1[i + 1] - d1[i] for i in range(3)]
    d3 = [d2[i + 1] - d2[i] for i in range(2)]
    d4 = d3[1] - d3[0]
    smooth = d4 - 5.0 * d2[1] + 30.0 * q[2]
    flux_before = None
    q, d1, d2, d3 = q[3:], d1[-1], d2[-1], d3[-1]
    edges = None
    for x in range(-1, x_size):
        q.append(cell(x + WIDTH))
        new1 = q[-1] - q[-2]
        new2 = new1 - d1
        new3 = new2 - d2
        new4 = new3 - d3
        new_smooth = new4 - 5.0 * d2 + 30.0 * q[0]
        speed = speed_x[x + 1, at, :]
        flux = speed * (smooth + new_smooth) - jnp.abs(speed) * (new4 - d4)
        d1, d2, d3, d4, smooth = new1, new2, new3, new4, new_smooth
        if x >= 0:
            row = row_here
            edge = rolled(halo, -(GROUP * x + WIDTH))
            around = [row if k == 0 else ahead(row, edge, lane, k) for k in range(-2, 4)]
            flux_y = combine(*around, speed_y[x, at, :])
            entry = rolled(seam_flux, -(GROUP * x + 2))
            below = jnp.where(lane == 0, entry, rolled(flux_y, 1))
            divergence = (flux - flux_before) + (flux_y - below)
            mapped = factor[pl.ds(x, 1), :]
            scale = mapped * mapped * (-1.0 / divisor)
            new = base(x) + scale * divergence
            store(x, at, new)
            edges = pack_edges(edges, new, x)
        flux_before = flux
        row_here = q[0]
        q = q[1:]
    return edges


def section_kernel(x_size, divisor, first, last, with_city, *refs):
    refs = list(refs)
    section = refs.pop(0)
    base_ref = section if first else refs.pop(0)
    west = [refs.pop(0) for _ in range(WIDTH)]
    east = [refs.pop(0) for _ in range(WIDTH)]
    south, north, own = [refs.pop(0) for _ in range(3)]
    speed_x, speed_y, speed_edge, factor = [refs.pop(0) for _ in range(4)]
    rows = south.shape[0]

    def strided(ref, t, x):
        start = pl.multiple_of(t * 8 * x_size, 8 * x_size)
        return ref.at[pl.ds(start + x, 8, stride=x_size), :]

    if last:
        if with_city:
            city = [refs.pop(0) for _ in range(6)]
            out, wall_out, indoor_out = refs
        else:
            refs.pop(0)
            (out,) = refs
    else:
        out, low, high, packed = refs

    def one(t, carry):
        def load(x, at):
            if first:
                return section[pl.ds(pl.multiple_of(t * 8 * x_size, 8 * x_size) + x, 8, stride=x_size), :]
            return section[x, at, :]

        def base(x):
            return base_ref[pl.ds(pl.multiple_of(t * 8 * x_size, 8 * x_size) + x, 8, stride=x_size), :]

        def store(x, at, new):
            if last:
                out[pl.ds(pl.multiple_of(t * 8 * x_size, 8 * x_size) + x, 8, stride=x_size), :] = new
                return
            out[x, at, :] = new
            if x < WIDTH:
                low[x, at, :] = new
            if x >= x_size - WIDTH:
                high[x - x_size + WIDTH, at, :] = new

        edges = section_tile(
            t, x_size, divisor, load, base, (west, east), (south, north, own), (speed_x, speed_y, speed_edge), factor, store
        )
        if not last:
            packed[pl.ds(pl.multiple_of(t * 8, 8), 8), :] = edges
        return carry

    lax.fori_loop(0, rows // 8, one, 0)
    if last and with_city:

        @pl.when(pl.program_id(0) == 0)
        def _():
            city_step(x_size, out, *city, wall_out, indoor_out)


def dot(a, b, dims):
    return lax.dot_general(
        a, b, (dims, ((), ())), precision=lax.Precision.HIGHEST, preferred_element_type=jnp.float32
    )


def city_step(x_size, out, counts, cols_ref, class_ref, table, wall_ref, indoor_ref, wall_out, indoor_out):
    deep = 16
    cols = cols_ref[...]
    slots = cols.shape[1]
    y_size = out.shape[1]
    cell_x = lax.div(cols, y_size)
    cell_y = lax.rem(cols, y_size)
    lower = [
        jnp.concatenate([out[pl.ds(8 * x_size * t + x, 8, stride=x_size), :] for t in range(deep // 8)], axis=0)
        for x in range(x_size)
    ]
    at_y = (lax.broadcasted_iota(jnp.int32, (y_size, slots), 0) == cell_y).astype(jnp.float32)
    gathered = dot(jnp.concatenate(lower, axis=0), at_y, ((1,), (0,)))
    air = jnp.zeros((deep, slots), jnp.float32)
    for x in range(x_size):
        air = jnp.where(cell_x == x, gathered[deep * x : deep * (x + 1)], air)
    air = air[:UL]
    onehot = (lax.broadcasted_iota(jnp.int32, (NCLS, slots), 0) == class_ref[...]).astype(jnp.float32)
    areas = dot(table[...], onehot, ((0,), (0,)))
    walls = wall_ref[...]
    indoor = indoor_ref[...]
    heat = heat_coef * areas * (walls[0:1] - air)
    wall_first = walls[0:1] - wall_coef * jnp.sum(heat, axis=0, keepdims=True) + conduct * (walls[1:2] - walls[0:1])
    middle = walls[1:-1] + conduct * (walls[:-2] - 2.0 * walls[1:-1] + walls[2:])
    last = walls[-1:] + conduct * (walls[-2:-1] - walls[-1:]) + inner_coef * (indoor - walls[-1:])
    indoor_new = indoor + room_coef * (walls[-1:] - indoor)
    live = lax.broadcasted_iota(jnp.int32, (1, slots), 1) < counts[0]
    wall_out[...] = jnp.where(live, jnp.concatenate([wall_first, middle, last], axis=0), walls)
    indoor_out[...] = jnp.where(live, indoor_new, indoor)
    heating = jnp.where(live, flux_coef * heat, 0.0)
    heating = jnp.concatenate([heating, jnp.zeros((deep - UL, slots), jnp.float32)], axis=0)
    spread = jnp.concatenate([jnp.where(cell_x == x, heating, 0.0) for x in range(x_size)], axis=0)
    added = dot(spread, at_y, ((1,), (1,)))
    for x in range(x_size):
        for t in range(deep // 8):
            out[pl.ds(8 * x_size * t + x, 8, stride=x_size), :] = (
                lower[x][8 * t : 8 * t + 8] + added[deep * x + 8 * t : deep * x + 8 * t + 8]
            )


def exchange(axis, low, high):
    size = lax.axis_size(axis)
    up = [(i, (i + 1) % size) for i in range(size)]
    down = [(j, i) for i, j in up]
    return lax.ppermute(high, axis, up), lax.ppermute(low, axis, down)


def per_device(
    scalars,
    winds,
    map_factor,
    urban_counts,
    urban_cols,
    street_class,
    area_table,
    wall_temp,
    indoor_temp,
):
    n_scalars, levels, x_size, y_size = scalars.shape
    slots = urban_cols.shape[0]
    rows = n_scalars * levels // CHUNKS
    f32 = functools.partial(jax.ShapeDtypeStruct, dtype=jnp.float32)
    field = scalars.reshape(n_scalars * levels * x_size, y_size)
    wind = winds.reshape(2 * levels * x_size, y_size)
    params = pltpu.CompilerParams(vmem_limit_bytes=40 * 2**20)
    whole = pl.BlockSpec(memory_space=pltpu.VMEM)

    lows, highs, packs = ([None] * CHUNKS for _ in range(3))
    for c in range(CHUNKS):
        extra = levels if c == 0 else 0
        lows[c], highs[c], packs[c] = pl.pallas_call(
            functools.partial(extract_kernel, None, x_size, c == 0),
            grid=(1,),
            in_specs=[pl.BlockSpec((rows * x_size, y_size), lambda g, c=c: (c, 0))] + [whole] * (c == 0),
            out_specs=[whole] * 3,
            out_shape=[
                f32((WIDTH * rows + extra, y_size)),
                f32((WIDTH * rows + extra, y_size)),
                f32((rows + extra, y_size)),
            ],
            compiler_params=params,
            name="extract",
        )(field, *([wind] if c == 0 else []))

    def swap(c):
        west, east = exchange("gx", lows[c], highs[c])
        south, north = exchange("gy", packs[c], packs[c])
        return west, east, south, north

    received = [swap(c) for c in range(CHUNKS)]
    west, east, south, north = received[0]
    edge_row = pl.BlockSpec((levels, y_size), lambda g: (WIDTH * rows // levels, 0))
    edge_pack = pl.BlockSpec((levels, y_size), lambda g: (rows // levels, 0))
    speeds = pl.pallas_call(
        functools.partial(wind_kernel, x_size),
        grid=(1,),
        in_specs=[whole, edge_row, edge_row, edge_pack, edge_pack, edge_pack],
        out_specs=[whole] * 3,
        out_shape=[f32((x_size + 1, levels, y_size)), f32((x_size, levels, y_size)), f32((levels, y_size))],
        compiler_params=params,
        name="speeds",
    )(wind, west, east, south, north, packs[0])

    block = levels
    steps = rows // block
    flat = pl.BlockSpec((block * x_size, y_size), lambda g: (g, 0))
    tall = pl.BlockSpec((x_size, block, y_size), lambda g: (0, g, 0))
    edge = pl.BlockSpec((WIDTH, block, y_size), lambda g: (0, g, 0))
    pack = pl.BlockSpec((block, y_size), lambda g: (g, 0))
    row_specs = [pl.BlockSpec((block, y_size), lambda g, j=j: (j * steps + g, 0)) for j in range(WIDTH)]
    flops = 3 * 45 * rows * x_size * y_size
    cost = pl.CostEstimate(flops=flops, bytes_accessed=16 * rows * x_size * y_size, transcendentals=0)
    sections = [None] * CHUNKS
    result = None
    for k, divisor in enumerate((3.0, 2.0, 1.0)):
        last = k == 2
        for c in range(CHUNKS):
            west, east, south, north = received[c]
            flat_c = pl.BlockSpec((block * x_size, y_size), lambda g, c=c: (c * steps + g, 0))
            operands = [field] if k == 0 else [sections[c], field]
            specs = [flat_c] if k == 0 else [tall, flat_c]
            operands += [west.reshape(-1, y_size)] * 3 + [east.reshape(-1, y_size)] * 3
            specs += row_specs * 2
            operands += [south, north, packs[c], *speeds, map_factor]
            specs += [pack] * 3 + [whole] * 4
            city = last and c == 0
            aliases = {}
            if city:
                operands += [
                    urban_counts,
                    urban_cols[None],
                    street_class[None],
                    area_table,
                    wall_temp,
                    indoor_temp[None],
                ]
                specs += [pl.BlockSpec(memory_space=pltpu.SMEM)] + [whole] * 5
                out_specs = [flat_c, whole, whole]
                out_shape = [f32(field.shape), f32(wall_temp.shape), f32((1, slots))]
            elif last:
                aliases = {len(operands): 0}
                operands += [result]
                specs += [pl.BlockSpec(memory_space=pl.ANY)]
                out_specs = [flat_c]
                out_shape = [f32(field.shape)]
            else:
                out_specs = [tall, edge, edge, pack]
                out_shape = [
                    f32((x_size, rows, y_size)),
                    f32((WIDTH, rows, y_size)),
                    f32((WIDTH, rows, y_size)),
                    f32((rows, y_size)),
                ]
            outs = pl.pallas_call(
                functools.partial(section_kernel, x_size, divisor, k == 0, last, city),
                grid=(steps,),
                in_specs=specs,
                out_specs=out_specs,
                out_shape=out_shape,
                input_output_aliases=aliases,
                compiler_params=params,
                cost_estimate=cost,
                name=f"section_{k}_{c}",
            )(*operands)
            if city:
                result, wall_out, indoor_out = outs
            elif last:
                (result,) = outs
            else:
                sections[c], lows[c], highs[c], packs[c] = outs
                received[c] = swap(c)
    return (result.reshape(scalars.shape), wall_out, indoor_out[0])


def solution(mesh):
    in_specs = (
        P(None, None, "gx", "gy"),
        P(None, None, "gx", "gy"),
        P("gx", "gy"),
        P(("gx", "gy")),
        P(("gx", "gy")),
        P(("gx", "gy")),
        P(),
        P(None, ("gx", "gy")),
        P(("gx", "gy")),
    )
    out_specs = (P(None, None, "gx", "gy"), P(None, ("gx", "gy")), P(("gx", "gy")))
    return jax.shard_map(
        per_device, mesh=mesh, in_specs=in_specs, out_specs=out_specs, check_vma=False
    )
```

time: 214 us -> 89.9 us (0.42)
  other arithmetic: 110 us -> 0 us
  Pallas kernels: 0 us -> 42.7 us
  local copies, waits for them, and re-layouts: 44.7 us -> 2.86 us
  waiting for transfers between devices: 33.1 us -> 12.8 us
  starting transfers between devices: 23.9 us -> 29.7 us
    sub x6 -> x0, other arithmetic: 64 us -> none  [face_divergence(): flux - jnp.abs(face_speed) * (shifted[5] - shifted[0] - 5.0 * (shifted[4]...]
    pallas_call x0 -> x9, Pallas kernels: none -> 42.7 us  [the longest x6 37.8 us: per_device(): pl.pallas_call(functools.partial(section_kernel, x_size, divisor, k == 0,...]
    add x5 -> x0, other arithmetic: 22 us -> none  [the longest x1 7.35 us: per_device(): advanced = scalars + section_rate(section_two)]
    ppermute x16 -> x24, waiting for transfers between devices: 33.1 us -> 12.8 us  [exchange(): return (lax.ppermute(high, axis, up), lax.ppermute(low, axis, down))]
    concatenate x4 -> x0, other arithmetic: 14.9 us -> none  [padded(): array = jnp.concatenate([before, array, after], axis=dim)]
    unnamed x59 -> x20, local copies, waits for them, and re-layouts: 17.7 us -> 2.86 us
    ppermute x8 -> x0, local copies, waits for them, and re-layouts: 12.4 us -> none  [the longest x4 7.04 us: padded(): before = lax.ppermute(last, axis, up)]
    slice x12 -> x0, local copies, waits for them, and re-layouts: 6.76 us -> none  [the longest x6 5.86 us: padded(): last = lax.slice_in_dim(array, length - width, length, axis=dim)]
  transfers between devices with their start and end apart: 16 -> 24, of which waited for: 5 -> 4; matrix products, arithmetic and copies ran while one was open for 24% -> 0% of each run, Pallas kernels for 0% -> 38%
where the time goes in v1:
time: 89.9 us; the launch traced here: 89.6 us
  Pallas kernels  42.7 us (47%)
  starting transfers between devices  29.7 us (33%)
  waiting for transfers between devices  12.8 us (14%)
  local copies, waits for them, and re-layouts  2.86 us (3%)
  between operations  1.53 us (2%)
    pallas_call x6, Pallas kernels, per_device(): pl.pallas_call(functools.partial(section_kernel, x_size, divisor, k == 0,...  37.8 us
    ppermute x24, starting transfers between devices, exchange(): return (lax.ppermute(high, axis, up), lax.ppermute(low, axis, down))  29.7 us
    ppermute x24, waiting for transfers between devices, exchange(): return (lax.ppermute(high, axis, up), lax.ppermute(low, axis, down))  12.8 us
    pallas_call x2, Pallas kernels, per_device(): pl.pallas_call(functools.partial(extract_kernel, None, x_size, c == 0), g...  3.62 us
    unnamed x20, local copies, waits for them, and re-layouts  2.86 us
  transfers between devices with their start and end apart: 24, of which 4 were waited for; matrix products, arithmetic and copies ran while one was open for 0% of the time, Pallas kernels for 38%

profile of v1, /device:TPU:0, one launch (start us, length us, event | category | flops | bytes accessed | tf_op | source)
XLA Modules:
  0.0 89.6 jit_solution(6641714624380947975)
XLA Ops:
  0.6 1.6 %copy-done = f32[4,64,16,128]{3,2,1,0:T(8,128)S(1)} copy-done((f32[4,64,16,128]{3,2,1,0:T(8,128)S(1)}, f32[4,64,16,128]{3,2,1,0:T(8,128)}, u32[]{:S(2)}) %copy-start) | copy-done | bytes 2097176
  2.2 1.2 %copy-done.2 = f32[2,64,16,128]{3,2,1,0:T(8,128)S(1)} copy-done((f32[2,64,16,128]{3,2,1,0:T(8,128)S(1)}, f32[2,64,16,128]{3,2,1,0:T(8,128)}, u32[]{:S(2)}) %copy-start.2) | copy-done | bytes 1048600
  3.5 2.2 %extract.3 = (f32[448,128]{1,0:T(8,128)S(1)}, f32[448,128]{1,0:T(8,128)S(1)}, f32[192,128]{1,0:T(8,128)S(1)}) custom-call(f32[4096,128]{1,0:T(8,128)S(1)} %bitcast.15, f32[2048,128]{1,0:T(8,128)S(1)} %bitcast.23), custom_call_target="tpu_custom_call" | custom-call | tf_op jit(solution)/shard_map/extract/pallas_call | solution.py:310
  5.7 3.1 %collective-permute-start.4 = (f32[448,128]{1,0:T(8,128)S(1)}, f32[448,128]{1,0:T(8,128)S(1)}, u32[]{:S(2)}, u32[]{:S(2)}) collective-permute-start(f32[448,128]{1,0:T(8,128)S(1)} %get-tuple-element.34), channel_id=1, source_target_pairs={{0,8},{8,16},{16,24},{24,0},{1,9},{9,17},{17,25},{25,1},{2,10},{10... | collective-permute-start | bytes 688136 | tf_op jit(solution)/shard_map/ppermute | solution.py:284
  8.7 2.1 %collective-permute-start.5 = (f32[448,128]{1,0:T(8,128)S(1)}, f32[448,128]{1,0:T(8,128)S(1)}, u32[]{:S(2)}, u32[]{:S(2)}) collective-permute-start(f32[448,128]{1,0:T(8,128)S(1)} %get-tuple-element.35), channel_id=1, source_target_pairs={{8,0},{16,8},{24,16},{0,24},{9,1},{17,9},{25,17},{1,25},{10,2},{18... | collective-permute-start | bytes 688136 | tf_op jit(solution)/shard_map/ppermute | solution.py:284
  10.8 1.6 %collective-permute-start.7 = (f32[192,128]{1,0:T(8,128)S(1)}, f32[192,128]{1,0:T(8,128)S(1)}, u32[]{:S(2)}, u32[]{:S(2)}) collective-permute-start(f32[192,128]{1,0:T(8,128)S(1)} %get-tuple-element.36.own.refs_9_), channel_id=1, source_target_pairs={{1,0},{2,1},{3,2},{4,3},{5,4},{6,5},{7,6},{0,7},{9,8},{10,9},{11,1... | collective-permute-start | bytes 294920 | tf_op jit(solution)/shard_map/ppermute | solution.py:284
  12.4 1.4 %extract.2 = (f32[384,128]{1,0:T(8,128)S(1)}, f32[384,128]{1,0:T(8,128)S(1)}, f32[128,128]{1,0:T(8,128)S(1)}) custom-call(f32[4096,128]{1,0:T(8,128)S(1)} %bitcast.16), custom_call_target="tpu_custom_call" | custom-call | tf_op jit(solution)/shard_map/extract/pallas_call | solution.py:310
  13.9 0.1 collective-permute-start
  14.0 1.1 %collective-permute-done.7.north.refs_8_ = f32[192,128]{1,0:T(8,128)S(1)} collective-permute-done((f32[192,128]{1,0:T(8,128)S(1)}, f32[192,128]{1,0:T(8,128)S(1)}, u32[]{:S(2)}, u32[]{:S(2)}) %collective-permute-start.7) | collective-permute-done | bytes 98336 | tf_op jit(solution)/shard_map/ppermute | solution.py:284
  15.1 2.7 %collective-permute-start.1 = (f32[384,128]{1,0:T(8,128)S(1)}, f32[384,128]{1,0:T(8,128)S(1)}, u32[]{:S(2)}, u32[]{:S(2)}) collective-permute-start(f32[384,128]{1,0:T(8,128)S(1)} %get-tuple-element.32), channel_id=1, source_target_pairs={{8,0},{16,8},{24,16},{0,24},{9,1},{17,9},{25,17},{1,25},{10,2},{18... | collective-permute-start | bytes 589832 | tf_op jit(solution)/shard_map/ppermute | solution.py:284
  17.8 2.1 %collective-permute-start.3 = (f32[128,128]{1,0:T(8,128)S(1)}, f32[128,128]{1,0:T(8,128)S(1)}, u32[]{:S(2)}, u32[]{:S(2)}) collective-permute-start(f32[128,128]{1,0:T(8,128)S(1)} %get-tuple-element.33.refs_9_), channel_id=1, source_target_pairs={{1,0},{2,1},{3,2},{4,3},{5,4},{6,5},{7,6},{0,7},{9,8},{10,9},{11,1... | collective-permute-start | bytes 196616 | tf_op jit(solution)/shard_map/ppermute | solution.py:284
  19.9 2.4 %collective-permute-done.5.east.refs_4_.refs_5_.refs_6_ = f32[448,128]{1,0:T(8,128)S(1)} collective-permute-done((f32[448,128]{1,0:T(8,128)S(1)}, f32[448,128]{1,0:T(8,128)S(1)}, u32[]{:S(2)}, u32[]{:S(2)}) %collective-permute-start.5) | collective-permute-done | bytes 229408 | tf_op jit(solution)/shard_map/ppermute | solution.py:284
  22.3 1.3 %speeds.1 = (f32[17,64,128]{2,1,0:T(8,128)S(1)}, f32[16,64,128]{2,1,0:T(8,128)S(1)}, f32[64,128]{1,0:T(8,128)S(1)}) custom-call(f32[2048,128]{1,0:T(8,128)S(1)} %bitcast.24, f32[448,128]{1,0:T(8,128)S(1)} %collective-permute-done.4.west.refs_1_.refs_2_.refs_3_, f32[448,128]{1,0:T(8,128)S(1)} %collective-permute-done.5.east.refs_4_.refs_5_.refs_6_, ...), custom_call_target="tpu_custom_call" | custom-call | tf_op jit(solution)/shard_map/speeds/pallas_call | solution.py:333
  23.6 6.1 %section_0_0.1 = (f32[16,128,128]{2,1,0:T(8,128)S(1)}, f32[3,128,128]{2,1,0:T(8,128)S(1)}, f32[3,128,128]{2,1,0:T(8,128)S(1)}, f32[128,128]{1,0:T(8,128)S(1)}) custom-call(f32[4096,128]{1,0:T(8,128)S(1)} %bitcast.17, f32[448,128]{1,0:T(8,128)S(1)} %collective-permute-done.4.west.refs_1_.refs_2_.refs_3_, ...), custom_call_target="tpu_custom_call" | custom-call | flops 35389440 | bytes 4194304 | tf_op jit(solution)/shard_map/section_0_0/pallas_call | solution.py:393
  29.8 0.5 collective-permute-start.16
  30.3 3.4 %collective-permute-start.17 = (f32[3,128,128]{2,1,0:T(8,128)S(1)}, f32[3,128,128]{2,1,0:T(8,128)S(1)}, u32[]{:S(2)}, u32[]{:S(2)}) collective-permute-start(f32[3,128,128]{2,1,0:T(8,128)S(1)} %get-tuple-element.50), channel_id=1, source_target_pairs={{8,0},{16,8},{24,16},{0,24},{9,1},{17,9},{25,17},{1,25},{10,2},{18... | collective-permute-start | bytes 589832 | tf_op jit(solution)/shard_map/ppermute | solution.py:284
  33.7 6.1 %section_0_1.1 = (f32[16,128,128]{2,1,0:T(8,128)S(1)}, f32[3,128,128]{2,1,0:T(8,128)S(1)}, f32[3,128,128]{2,1,0:T(8,128)S(1)}, f32[128,128]{1,0:T(8,128)S(1)}) custom-call(f32[4096,128]{1,0:T(8,128)S(1)} %bitcast.18, f32[384,128]{1,0:T(8,128)S(1)} %collective-permute-done.refs_1_.refs_2_.refs_3_, ...), custom_call_target="tpu_custom_call" | custom-call | flops 35389440 | bytes 4194304 | tf_op jit(solution)/shard_map/section_0_1/pallas_call | solution.py:393
  39.8 0.2 collective-permute-start.8
  40.0 3.7 %collective-permute-start.9 = (f32[3,128,128]{2,1,0:T(8,128)S(1)}, f32[3,128,128]{2,1,0:T(8,128)S(1)}, u32[]{:S(2)}, u32[]{:S(2)}) collective-permute-start(f32[3,128,128]{2,1,0:T(8,128)S(1)} %get-tuple-element.42), channel_id=1, source_target_pairs={{8,0},{16,8},{24,16},{0,24},{9,1},{17,9},{25,17},{1,25},{10,2},{18... | collective-permute-start | bytes 589832 | tf_op jit(solution)/shard_map/ppermute | solution.py:284
  43.7 4.6 %collective-permute-done.18.refs_8_ = f32[128,128]{1,0:T(8,128)S(1)} collective-permute-done((f32[128,128]{1,0:T(8,128)S(1)}, f32[128,128]{1,0:T(8,128)S(1)}, u32[]{:S(2)}, u32[]{:S(2)}) %collective-permute-start.18) | collective-permute-done | bytes 65568 | tf_op jit(solution)/shard_map/ppermute | solution.py:284
  48.3 0.5 collective-permute-start.10
  48.8 6.2 %section_1_0.1 = (f32[16,128,128]{2,1,0:T(8,128)S(1)}, f32[3,128,128]{2,1,0:T(8,128)S(1)}, f32[3,128,128]{2,1,0:T(8,128)S(1)}, f32[128,128]{1,0:T(8,128)S(1)}) custom-call(f32[16,128,128]{2,1,0:T(8,128)S(1)} %get-tuple-element.48.refs_0_, f32[4096,128]{1,0:T(8,128)S(1)} %bitcast.19, f32[384,128]{1,0:T(8,128)S(1)} %bitcast.31, f32[384,128]{1,0:T(8,128)S(1)} %bitcast.32, ...), custom_call_target="tpu_custom_call" | custom-call | flops 35389440 | bytes 4194304 | tf_op jit(solution)/shard_map/section_1_0/pallas_call | solution.py:393
  55.0 0.1 collective-permute-start.20
  55.0 3.8 %collective-permute-start.21 = (f32[3,128,128]{2,1,0:T(8,128)S(1)}, f32[3,128,128]{2,1,0:T(8,128)S(1)}, u32[]{:S(2)}, u32[]{:S(2)}) collective-permute-start(f32[3,128,128]{2,1,0:T(8,128)S(1)} %get-tuple-element.54), channel_id=1, source_target_pairs={{8,0},{16,8},{24,16},{0,24},{9,1},{17,9},{25,17},{1,25},{10,2},{18... | collective-permute-start | bytes 589832 | tf_op jit(solution)/shard_map/ppermute | solution.py:284
  58.9 1.6 %collective-permute-start.23 = (f32[128,128]{1,0:T(8,128)S(1)}, f32[128,128]{1,0:T(8,128)S(1)}, u32[]{:S(2)}, u32[]{:S(2)}) collective-permute-start(f32[128,128]{1,0:T(8,128)S(1)} %get-tuple-element.55.refs_10_), channel_id=1, source_target_pairs={{1,0},{2,1},{3,2},{4,3},{5,4},{6,5},{7,6},{0,7},{9,8},{10,9},{11,1... | collective-permute-start | bytes 196616 | tf_op jit(solution)/shard_map/ppermute | solution.py:284
  60.5 6.2 %section_1_1.1 = (f32[16,128,128]{2,1,0:T(8,128)S(1)}, f32[3,128,128]{2,1,0:T(8,128)S(1)}, f32[3,128,128]{2,1,0:T(8,128)S(1)}, f32[128,128]{1,0:T(8,128)S(1)}) custom-call(f32[16,128,128]{2,1,0:T(8,128)S(1)} %get-tuple-element.40.refs_0_, f32[4096,128]{1,0:T(8,128)S(1)} %bitcast.20, f32[384,128]{1,0:T(8,128)S(1)} %bitcast.25, f32[384,128]{1,0:T(8,128)S(1)} %bitcast.26, ...), custom_call_target="tpu_custom_call" | custom-call | flops 35389440 | bytes 4194304 | tf_op jit(solution)/shard_map/section_1_1/pallas_call | solution.py:393
  66.7 0.1 collective-permute-start.12
  66.8 3.8 %collective-permute-start.13 = (f32[3,128,128]{2,1,0:T(8,128)S(1)}, f32[3,128,128]{2,1,0:T(8,128)S(1)}, u32[]{:S(2)}, u32[]{:S(2)}) collective-permute-start(f32[3,128,128]{2,1,0:T(8,128)S(1)} %get-tuple-element.46), channel_id=1, source_target_pairs={{8,0},{16,8},{24,16},{0,24},{9,1},{17,9},{25,17},{1,25},{10,2},{18... | collective-permute-start | bytes 589832 | tf_op jit(solution)/shard_map/ppermute | solution.py:284
  70.6 4.6 %collective-permute-done.22.refs_8_ = f32[128,128]{1,0:T(8,128)S(1)} collective-permute-done((f32[128,128]{1,0:T(8,128)S(1)}, f32[128,128]{1,0:T(8,128)S(1)}, u32[]{:S(2)}, u32[]{:S(2)}) %collective-permute-start.22) | collective-permute-done | bytes 65568 | tf_op jit(solution)/shard_map/ppermute | solution.py:284
  75.2 0.5 collective-permute-start.14
  76.4 7.1 %section_2_0.1 = (f32[4096,128]{1,0:T(8,128)}, f32[10,256]{1,0:T(8,128)}, f32[1,256]{1,0:T(1,128)}) custom-call(f32[16,128,128]{2,1,0:T(8,128)S(1)} %get-tuple-element.52.refs_0_, f32[4096,128]{1,0:T(8,128)S(1)} %bitcast.21, f32[384,128]{1,0:T(8,128)S(1)} %bitcast.28, f32[384,128]{1,0:T(8,128)S(1)} %bitcast.29, f32[384,128]{1,0:T(8,128)S(1)} %bitcast.30, ...), custom_call_target="tpu_custom_call" | custom-call | flops 35389440 | bytes 4194304 | tf_op jit(solution)/shard_map/section_2_0/pallas_call | solution.py:393
  83.5 6.1 %section_2_1.1 = f32[4096,128]{1,0:T(8,128)} custom-call(f32[16,128,128]{2,1,0:T(8,128)S(1)} %get-tuple-element.44.refs_0_, f32[4096,128]{1,0:T(8,128)S(1)} %bitcast.22, f32[384,128]{1,0:T(8,128)S(1)} %bitcast.43, f32[384,128]{1,0:T(8,128)S(1)} %bitcast.44, f32[384,128]{1,0:T(8,128)S(1)} %bitcast.45, ...), custom_call_target="tpu_custom_call", output_to_operand_aliasing={{}: (15, {})} | custom-call | flops 35389440 | bytes 4194304 | tf_op jit(solution)/shard_map/section_2_1/pallas_call | solution.py:393
  (45 shorter events, 0.1 us)
Async XLA Ops:
  3.4 18.9 %copy-start.3 = (f32[2,64,16,128]{3,2,1,0:T(8,128)S(1)}, f32[2,64,16,128]{3,2,1,0:T(8,128)}, u32[]{:S(2)}) copy-start(f32[2,64,16,128]{3,2,1,0:T(8,128)} %param.10) | copy-start | bytes 3145732
  5.6 18.0 %copy-start.1 = (f32[4,64,16,128]{3,2,1,0:T(8,128)S(1)}, f32[4,64,16,128]{3,2,1,0:T(8,128)}, u32[]{:S(2)}) copy-start(f32[4,64,16,128]{3,2,1,0:T(8,128)} %param.9) | copy-start | bytes 6291460
  5.6 18.0 %copy-start.4 = (f32[16,128]{1,0:T(8,128)S(1)}, f32[16,128]{1,0:T(8,128)}, u32[]{:S(2)}) copy-start(f32[16,128]{1,0:T(8,128)} %refs_14_.7) | copy-start | bytes 24580
  5.7 14.2 %collective-permute-start.4 = (f32[448,128]{1,0:T(8,128)S(1)}, f32[448,128]{1,0:T(8,128)S(1)}, u32[]{:S(2)}, u32[]{:S(2)}) collective-permute-start(f32[448,128]{1,0:T(8,128)S(1)} %get-tuple-element.34), channel_id=1, source_target_pairs={{0,8},{8,16},{16,24},{24,0},{1,9},{9,17},{17,25},{25,1},{2,10},{10... | collective-permute-start | bytes 688136 | tf_op jit(solution)/shard_map/ppermute | solution.py:284
  8.7 13.6 %collective-permute-start.5 = (f32[448,128]{1,0:T(8,128)S(1)}, f32[448,128]{1,0:T(8,128)S(1)}, u32[]{:S(2)}, u32[]{:S(2)}) collective-permute-start(f32[448,128]{1,0:T(8,128)S(1)} %get-tuple-element.35), channel_id=1, source_target_pairs={{8,0},{16,8},{24,16},{0,24},{9,1},{17,9},{25,17},{1,25},{10,2},{18... | collective-permute-start | bytes 688136 | tf_op jit(solution)/shard_map/ppermute | solution.py:284
  10.8 4.3 %collective-permute-start.7 = (f32[192,128]{1,0:T(8,128)S(1)}, f32[192,128]{1,0:T(8,128)S(1)}, u32[]{:S(2)}, u32[]{:S(2)}) collective-permute-start(f32[192,128]{1,0:T(8,128)S(1)} %get-tuple-element.36.own.refs_9_), channel_id=1, source_target_pairs={{1,0},{2,1},{3,2},{4,3},{5,4},{6,5},{7,6},{0,7},{9,8},{10,9},{11,1... | collective-permute-start | bytes 294920 | tf_op jit(solution)/shard_map/ppermute | solution.py:284
  12.4 5.3 %collective-permute-start.6 = (f32[192,128]{1,0:T(8,128)S(1)}, f32[192,128]{1,0:T(8,128)S(1)}, u32[]{:S(2)}, u32[]{:S(2)}) collective-permute-start(f32[192,128]{1,0:T(8,128)S(1)} %get-tuple-element.36.own.refs_9_), channel_id=1, source_target_pairs={{0,1},{1,2},{2,3},{3,4},{4,5},{5,6},{6,7},{7,0},{8,9},{9,10},{10,1... | collective-permute-start | bytes 294920 | tf_op jit(solution)/shard_map/ppermute | solution.py:284
  13.9 19.8 %collective-permute-start = (f32[384,128]{1,0:T(8,128)S(1)}, f32[384,128]{1,0:T(8,128)S(1)}, u32[]{:S(2)}, u32[]{:S(2)}) collective-permute-start(f32[384,128]{1,0:T(8,128)S(1)} %get-tuple-element.31), channel_id=1, source_target_pairs={{0,8},{8,16},{16,24},{24,0},{1,9},{9,17},{17,25},{25,1},{2,10},{10... | collective-permute-start | bytes 589832 | tf_op jit(solution)/shard_map/ppermute | solution.py:284
  15.1 18.6 %collective-permute-start.1 = (f32[384,128]{1,0:T(8,128)S(1)}, f32[384,128]{1,0:T(8,128)S(1)}, u32[]{:S(2)}, u32[]{:S(2)}) collective-permute-start(f32[384,128]{1,0:T(8,128)S(1)} %get-tuple-element.32), channel_id=1, source_target_pairs={{8,0},{16,8},{24,16},{0,24},{9,1},{17,9},{25,17},{1,25},{10,2},{18... | collective-permute-start | bytes 589832 | tf_op jit(solution)/shard_map/ppermute | solution.py:284
  17.8 12.5 %collective-permute-start.3 = (f32[128,128]{1,0:T(8,128)S(1)}, f32[128,128]{1,0:T(8,128)S(1)}, u32[]{:S(2)}, u32[]{:S(2)}) collective-permute-start(f32[128,128]{1,0:T(8,128)S(1)} %get-tuple-element.33.refs_9_), channel_id=1, source_target_pairs={{1,0},{2,1},{3,2},{4,3},{5,4},{6,5},{7,6},{0,7},{9,8},{10,9},{11,1... | collective-permute-start | bytes 196616 | tf_op jit(solution)/shard_map/ppermute | solution.py:284
  19.9 13.8 %collective-permute-start.2 = (f32[128,128]{1,0:T(8,128)S(1)}, f32[128,128]{1,0:T(8,128)S(1)}, u32[]{:S(2)}, u32[]{:S(2)}) collective-permute-start(f32[128,128]{1,0:T(8,128)S(1)} %get-tuple-element.33.refs_9_), channel_id=1, source_target_pairs={{0,1},{1,2},{2,3},{3,4},{4,5},{5,6},{6,7},{7,0},{8,9},{9,10},{10,1... | collective-permute-start | bytes 196616 | tf_op jit(solution)/shard_map/ppermute | solution.py:284
  29.8 18.5 %collective-permute-start.16 = (f32[3,128,128]{2,1,0:T(8,128)S(1)}, f32[3,128,128]{2,1,0:T(8,128)S(1)}, u32[]{:S(2)}, u32[]{:S(2)}) collective-permute-start(f32[3,128,128]{2,1,0:T(8,128)S(1)} %get-tuple-element.49), channel_id=1, source_target_pairs={{0,8},{8,16},{16,24},{24,0},{1,9},{9,17},{17,25},{25,1},{2,10},{10... | collective-permute-start | bytes 589832 | tf_op jit(solution)/shard_map/ppermute | solution.py:284
  30.3 18.5 %collective-permute-start.17 = (f32[3,128,128]{2,1,0:T(8,128)S(1)}, f32[3,128,128]{2,1,0:T(8,128)S(1)}, u32[]{:S(2)}, u32[]{:S(2)}) collective-permute-start(f32[3,128,128]{2,1,0:T(8,128)S(1)} %get-tuple-element.50), channel_id=1, source_target_pairs={{8,0},{16,8},{24,16},{0,24},{9,1},{17,9},{25,17},{1,25},{10,2},{18... | collective-permute-start | bytes 589832 | tf_op jit(solution)/shard_map/ppermute | solution.py:284
  33.6 10.0 %collective-permute-start.19 = (f32[128,128]{1,0:T(8,128)S(1)}, f32[128,128]{1,0:T(8,128)S(1)}, u32[]{:S(2)}, u32[]{:S(2)}) collective-permute-start(f32[128,128]{1,0:T(8,128)S(1)} %get-tuple-element.51.refs_10_), channel_id=1, source_target_pairs={{1,0},{2,1},{3,2},{4,3},{5,4},{6,5},{7,6},{0,7},{9,8},{10,9},{11,1... | collective-permute-start | bytes 196616 | tf_op jit(solution)/shard_map/ppermute | solution.py:284
  39.8 20.7 %collective-permute-start.8 = (f32[3,128,128]{2,1,0:T(8,128)S(1)}, f32[3,128,128]{2,1,0:T(8,128)S(1)}, u32[]{:S(2)}, u32[]{:S(2)}) collective-permute-start(f32[3,128,128]{2,1,0:T(8,128)S(1)} %get-tuple-element.41), channel_id=1, source_target_pairs={{0,8},{8,16},{16,24},{24,0},{1,9},{9,17},{17,25},{25,1},{2,10},{10... | collective-permute-start | bytes 589832 | tf_op jit(solution)/shard_map/ppermute | solution.py:284
  40.0 20.5 %collective-permute-start.9 = (f32[3,128,128]{2,1,0:T(8,128)S(1)}, f32[3,128,128]{2,1,0:T(8,128)S(1)}, u32[]{:S(2)}, u32[]{:S(2)}) collective-permute-start(f32[3,128,128]{2,1,0:T(8,128)S(1)} %get-tuple-element.42), channel_id=1, source_target_pairs={{8,0},{16,8},{24,16},{0,24},{9,1},{17,9},{25,17},{1,25},{10,2},{18... | collective-permute-start | bytes 589832 | tf_op jit(solution)/shard_map/ppermute | solution.py:284
  43.7 4.6 %collective-permute-start.18 = (f32[128,128]{1,0:T(8,128)S(1)}, f32[128,128]{1,0:T(8,128)S(1)}, u32[]{:S(2)}, u32[]{:S(2)}) collective-permute-start(f32[128,128]{1,0:T(8,128)S(1)} %get-tuple-element.51.refs_10_), channel_id=1, source_target_pairs={{0,1},{1,2},{2,3},{3,4},{4,5},{5,6},{6,7},{7,0},{8,9},{9,10},{10,1... | collective-permute-start | bytes 196616 | tf_op jit(solution)/shard_map/ppermute | solution.py:284
  48.3 6.8 %collective-permute-start.11 = (f32[128,128]{1,0:T(8,128)S(1)}, f32[128,128]{1,0:T(8,128)S(1)}, u32[]{:S(2)}, u32[]{:S(2)}) collective-permute-start(f32[128,128]{1,0:T(8,128)S(1)} %get-tuple-element.43.refs_10_), channel_id=1, source_target_pairs={{1,0},{2,1},{3,2},{4,3},{5,4},{6,5},{7,6},{0,7},{9,8},{10,9},{11,1... | collective-permute-start | bytes 196616 | tf_op jit(solution)/shard_map/ppermute | solution.py:284
  48.3 10.6 %collective-permute-start.10 = (f32[128,128]{1,0:T(8,128)S(1)}, f32[128,128]{1,0:T(8,128)S(1)}, u32[]{:S(2)}, u32[]{:S(2)}) collective-permute-start(f32[128,128]{1,0:T(8,128)S(1)} %get-tuple-element.43.refs_10_), channel_id=1, source_target_pairs={{0,1},{1,2},{2,3},{3,4},{4,5},{5,6},{6,7},{7,0},{8,9},{9,10},{10,1... | collective-permute-start | bytes 196616 | tf_op jit(solution)/shard_map/ppermute | solution.py:284
  55.0 20.2 %collective-permute-start.20 = (f32[3,128,128]{2,1,0:T(8,128)S(1)}, f32[3,128,128]{2,1,0:T(8,128)S(1)}, u32[]{:S(2)}, u32[]{:S(2)}) collective-permute-start(f32[3,128,128]{2,1,0:T(8,128)S(1)} %get-tuple-element.53), channel_id=1, source_target_pairs={{0,8},{8,16},{16,24},{24,0},{1,9},{9,17},{17,25},{25,1},{2,10},{10... | collective-permute-start | bytes 589832 | tf_op jit(solution)/shard_map/ppermute | solution.py:284
  55.0 21.3 %collective-permute-start.21 = (f32[3,128,128]{2,1,0:T(8,128)S(1)}, f32[3,128,128]{2,1,0:T(8,128)S(1)}, u32[]{:S(2)}, u32[]{:S(2)}) collective-permute-start(f32[3,128,128]{2,1,0:T(8,128)S(1)} %get-tuple-element.54), channel_id=1, source_target_pairs={{8,0},{16,8},{24,16},{0,24},{9,1},{17,9},{25,17},{1,25},{10,2},{18... | collective-permute-start | bytes 589832 | tf_op jit(solution)/shard_map/ppermute | solution.py:284
  58.9 11.7 %collective-permute-start.23 = (f32[128,128]{1,0:T(8,128)S(1)}, f32[128,128]{1,0:T(8,128)S(1)}, u32[]{:S(2)}, u32[]{:S(2)}) collective-permute-start(f32[128,128]{1,0:T(8,128)S(1)} %get-tuple-element.55.refs_10_), channel_id=1, source_target_pairs={{1,0},{2,1},{3,2},{4,3},{5,4},{6,5},{7,6},{0,7},{9,8},{10,9},{11,1... | collective-permute-start | bytes 196616 | tf_op jit(solution)/shard_map/ppermute | solution.py:284
  60.4 15.9 %copy-start.5 = (f32[10,256]{1,0:T(8,128)S(1)}, f32[10,256]{1,0:T(8,128)}, u32[]{:S(2)}) copy-start(f32[10,256]{1,0:T(8,128)} %refs_19_.1) | copy-start | bytes 30724
  60.4 15.9 %copy-start.6 = (f32[10,10]{1,0:T(8,128)S(1)}, f32[10,10]{1,0:T(8,128)}, u32[]{:S(2)}) copy-start(f32[10,10]{1,0:T(8,128)} %refs_18_.1) | copy-start | bytes 1204
  60.5 15.9 %copy-start.7 = (s32[256]{0:T(256)S(1)}, s32[256]{0:T(256)}, u32[]{:S(2)}) copy-start(s32[256]{0:T(256)} %param.13) | copy-start | bytes 3076
  60.5 15.9 %copy-start.8 = (s32[256]{0:T(256)S(1)}, s32[256]{0:T(256)}, u32[]{:S(2)}) copy-start(s32[256]{0:T(256)} %param.14) | copy-start | bytes 3076
  60.5 15.9 %copy-start.9 = (f32[256]{0:T(256)S(1)}, f32[256]{0:T(256)}, u32[]{:S(2)}) copy-start(f32[256]{0:T(256)} %param.17) | copy-start | bytes 3076
  66.7 16.8 %collective-permute-start.12 = (f32[3,128,128]{2,1,0:T(8,128)S(1)}, f32[3,128,128]{2,1,0:T(8,128)S(1)}, u32[]{:S(2)}, u32[]{:S(2)}) collective-permute-start(f32[3,128,128]{2,1,0:T(8,128)S(1)} %get-tuple-element.45), channel_id=1, source_target_pairs={{0,8},{8,16},{16,24},{24,0},{1,9},{9,17},{17,25},{25,1},{2,10},{10... | collective-permute-start | bytes 589832 | tf_op jit(solution)/shard_map/ppermute | solution.py:284
  66.8 16.8 %collective-permute-start.13 = (f32[3,128,128]{2,1,0:T(8,128)S(1)}, f32[3,128,128]{2,1,0:T(8,128)S(1)}, u32[]{:S(2)}, u32[]{:S(2)}) collective-permute-start(f32[3,128,128]{2,1,0:T(8,128)S(1)} %get-tuple-element.46), channel_id=1, source_target_pairs={{8,0},{16,8},{24,16},{0,24},{9,1},{17,9},{25,17},{1,25},{10,2},{18... | collective-permute-start | bytes 589832 | tf_op jit(solution)/shard_map/ppermute | solution.py:284
  70.6 4.6 %collective-permute-start.22 = (f32[128,128]{1,0:T(8,128)S(1)}, f32[128,128]{1,0:T(8,128)S(1)}, u32[]{:S(2)}, u32[]{:S(2)}) collective-permute-start(f32[128,128]{1,0:T(8,128)S(1)} %get-tuple-element.55.refs_10_), channel_id=1, source_target_pairs={{0,1},{1,2},{2,3},{3,4},{4,5},{5,6},{6,7},{7,0},{8,9},{9,10},{10,1... | collective-permute-start | bytes 196616 | tf_op jit(solution)/shard_map/ppermute | solution.py:284
  75.2 8.4 %collective-permute-start.15 = (f32[128,128]{1,0:T(8,128)S(1)}, f32[128,128]{1,0:T(8,128)S(1)}, u32[]{:S(2)}, u32[]{:S(2)}) collective-permute-start(f32[128,128]{1,0:T(8,128)S(1)} %get-tuple-element.47.refs_10_), channel_id=1, source_target_pairs={{1,0},{2,1},{3,2},{4,3},{5,4},{6,5},{7,6},{0,7},{9,8},{10,9},{11,1... | collective-permute-start | bytes 196616 | tf_op jit(solution)/shard_map/ppermute | solution.py:284
  75.2 8.3 %collective-permute-start.14 = (f32[128,128]{1,0:T(8,128)S(1)}, f32[128,128]{1,0:T(8,128)S(1)}, u32[]{:S(2)}, u32[]{:S(2)}) collective-permute-start(f32[128,128]{1,0:T(8,128)S(1)} %get-tuple-element.47.refs_10_), channel_id=1, source_target_pairs={{0,1},{1,2},{2,3},{3,4},{4,5},{5,6},{6,7},{7,0},{8,9},{9,10},{10,1... | collective-permute-start | bytes 196616 | tf_op jit(solution)/shard_map/ppermute | solution.py:284
  (2 other events, 2.8 us)

commit v2 on v1

--- a/solution.py
+++ b/solution.py
@@ -2,6 +2,8 @@
 
 import jax
 import jax.numpy as jnp
+import ml_dtypes
+import numpy as np
 from jax import lax
 from jax.experimental import pallas as pl
 from jax.experimental.pallas import tpu as pltpu
@@ -13,6 +15,10 @@
 WIDTH = 3
 GROUP = 8
 CHUNKS = 2
+PIECE = 256
+DIVISORS = (3.0, 2.0, 1.0)
+HIGH = (1, -8, 37, 37, -8, 1)
+DAMP = (-1, 5, -10, 10, -5, 1)
 
 heat_coef = 0.5
 wall_coef = 0.05
@@ -42,12 +48,6 @@
     if k > 0:
         return rolled(jnp.where(lane < k, halo, row), -k)
     return rolled(jnp.where(lane >= row.shape[1] + k, halo, row), -k)
-
-
-def combine(a, b, c, d, e, f, speed):
-    high = 37.0 * (c + d) - 8.0 * (b + e) + (a + f)
-    damp = (f - a) - 5.0 * (e - b) + 10.0 * (d - c)
-    return speed * high - jnp.abs(speed) * damp
 
 
 def extract_kernel(tiles, x_size, with_wind, *refs):
@@ -90,8 +90,12 @@
         lax.fori_loop(0, levels // 8, one_wind, 0)
 
 
-def wind_kernel(x_size, wind, west, east, south, north, own, speed_x, speed_y, speed_edge):
+def wind_kernel(x_size, wind, factor, west, east, south, north, speed_x, ahead_y, behind_y, edge_ahead, edge_behind, scales):
     levels = speed_x.shape[1]
+    for x in range(x_size):
+        mapped = factor[pl.ds(x, 1), :]
+        for k, divisor in enumerate(DIVISORS):
+            scales[k, x] = jnp.broadcast_to(mapped * mapped * (-1.0 / divisor), scales.shape[2:])
 
     def one(t, carry):
         base = pl.multiple_of(t * 8 * x_size, 8 * x_size)
@@ -105,88 +109,63 @@
         lane = lane_index(before.shape)
         first = (lane & (GROUP - 1)) < WIDTH
         halo = jnp.where(first, south[at, :], north[at, :])
+        forward, backward = None, None
         for x in range(x_size):
             row = wind[pl.ds(base + x, 8, stride=x_size), :]
             edge = rolled(halo, -(GROUP * x + WIDTH))
-            speed_y[x, at, :] = face_scale * (row + ahead(row, edge, lane, 1))
-        seam = jnp.where(first, south[at, :], own[at, :])
-        speed_edge[at, :] = face_scale * (seam + rolled(seam, -1))
+            front = face_scale * (row + ahead(row, edge, lane, 1))
+            back = face_scale * (row + ahead(row, edge, lane, -1))
+            ahead_y[x, at, :] = front
+            behind_y[x, at, :] = back
+            forward = pack_edges(forward, front, x)
+            backward = pack_edges(backward, back, x)
+        edge_ahead[at, :] = forward
+        edge_behind[at, :] = backward
         return carry
 
     lax.fori_loop(0, levels // 8, one, 0)
 
 
-def section_tile(t, x_size, divisor, load, base, halos, packs, speeds, factor, store):
-    west, east = halos
-    south, north, own = packs
-    speed_x, speed_y, speed_edge = speeds
-    at = pl.ds(pl.multiple_of(t * 8, 8), 8)
-    south_edges = south[at, :]
-    lane = lane_index(south_edges.shape)
-    first = (lane & (GROUP - 1)) < WIDTH
-    halo = jnp.where(first, south_edges, north[at, :])
-    seam = jnp.where(first, south_edges, own[at, :])
-    seam_flux = combine(*[rolled(seam, -k) for k in range(-2, 4)], speed_edge[at, :])
-
-    def cell(x):
-        if x < 0:
-            return west[x + WIDTH][at, :]
-        if x >= x_size:
-            return east[x - x_size][at, :]
-        return load(x, at)
-
-    q = [cell(x) for x in range(-3, 2)]
-    d1 = [q[i + 1] - q[i] for i in range(4)]
-    d2 = [d1[i + 1] - d1[i] for i in range(3)]
-    d3 = [d2[i + 1] - d2[i] for i in range(2)]
-    d4 = d3[1] - d3[0]
-    smooth = d4 - 5.0 * d2[1] + 30.0 * q[2]
-    flux_before = None
-    q, d1, d2, d3 = q[3:], d1[-1], d2[-1], d3[-1]
-    edges = None
-    for x in range(-1, x_size):
-        q.append(cell(x + WIDTH))
-        new1 = q[-1] - q[-2]
-        new2 = new1 - d1
-        new3 = new2 - d2
-        new4 = new3 - d3
-        new_smooth = new4 - 5.0 * d2 + 30.0 * q[0]
-        speed = speed_x[x + 1, at, :]
-        flux = speed * (smooth + new_smooth) - jnp.abs(speed) * (new4 - d4)
-        d1, d2, d3, d4, smooth = new1, new2, new3, new4, new_smooth
-        if x >= 0:
-            row = row_here
-            edge = rolled(halo, -(GROUP * x + WIDTH))
-            around = [row if k == 0 else ahead(row, edge, lane, k) for k in range(-2, 4)]
-            flux_y = combine(*around, speed_y[x, at, :])
-            entry = rolled(seam_flux, -(GROUP * x + 2))
-            below = jnp.where(lane == 0, entry, rolled(flux_y, 1))
-            divergence = (flux - flux_before) + (flux_y - below)
-            mapped = factor[pl.ds(x, 1), :]
-            scale = mapped * mapped * (-1.0 / divisor)
-            new = base(x) + scale * divergence
-            store(x, at, new)
-            edges = pack_edges(edges, new, x)
-        flux_before = flux
-        row_here = q[0]
-        q = q[1:]
-    return edges
-
-
-def section_kernel(x_size, divisor, first, last, with_city, *refs):
+def stencil_matrices(y_size):
+    inner = np.zeros((y_size, 4 * y_size), np.float32)
+    edges = np.zeros((y_size, 4 * y_size), np.float32)
+    for part, (taps, offset) in enumerate(((HIGH, -2), (DAMP, -2), (HIGH, -3), (DAMP, -3))):
+        for n, tap in enumerate(taps):
+            k = n + offset
+            for j in range(y_size):
+                if 0 <= j + k < y_size:
+                    inner[j + k, part * y_size + j] = tap
+            for g in range(0, y_size, GROUP):
+                for j in range(WIDTH):
+                    if j + k < 0:
+                        edges[g + WIDTH + j + k, part * y_size + g + WIDTH + j] = tap
+                    if j - WIDTH + k >= 0:
+                        edges[g + j + k, part * y_size + g + j] = tap
+    return [jnp.asarray(np.concatenate([m, m]).astype(ml_dtypes.bfloat16)) for m in (inner, edges)]
+
+
+def stencil_product(values, matrix):
+    leading = values.astype(jnp.bfloat16)
+    trailing = (values - leading.astype(jnp.float32)).astype(jnp.bfloat16)
+    return jnp.dot(
+        jnp.concatenate([leading, trailing], axis=1), matrix[...], preferred_element_type=jnp.float32
+    )
+
+
+def section_kernel(x_size, k, last, with_city, *refs):
     refs = list(refs)
+    first = k == 0
     section = refs.pop(0)
     base_ref = section if first else refs.pop(0)
     west = [refs.pop(0) for _ in range(WIDTH)]
     east = [refs.pop(0) for _ in range(WIDTH)]
-    south, north, own = [refs.pop(0) for _ in range(3)]
-    speed_x, speed_y, speed_edge, factor = [refs.pop(0) for _ in range(4)]
-    rows = south.shape[0]
-
-    def strided(ref, t, x):
-        start = pl.multiple_of(t * 8 * x_size, 8 * x_size)
-        return ref.at[pl.ds(start + x, 8, stride=x_size), :]
-
+    south, north = [refs.pop(0) for _ in range(2)]
+    speed_x, ahead_y, behind_y, edge_ahead, edge_behind, scales = [refs.pop(0) for _ in range(6)]
+    inner_matrix, edge_matrix = [refs.pop(0) for _ in range(2)]
+    parts = refs[-4:]
+    share = refs[-5]
+    refs = refs[:-5]
+    rows, y_size = south.shape
     if last:
         if with_city:
             city = [refs.pop(0) for _ in range(6)]
@@ -197,30 +176,91 @@
     else:
         out, low, high, packed = refs
 
+    total = rows * x_size
+    piece = PIECE
+    for p in range(total // piece):
+        if first:
+            values = section[p * piece : (p + 1) * piece, :]
+        else:
+            n = piece // rows
+            values = section[p * n : (p + 1) * n].reshape(piece, y_size)
+        product = stencil_product(values, inner_matrix)
+        for j, part in enumerate(parts):
+            part[p * piece : (p + 1) * piece, :] = product[:, j * y_size : (j + 1) * y_size]
+    lane = lane_index((rows, y_size))
+    halo = jnp.where((lane & (GROUP - 1)) < WIDTH, south[...], north[...])
+    product = stencil_product(halo, edge_matrix)
+    after, before = edge_ahead[...], edge_behind[...]
+    share[...] = (
+        after * product[:, :y_size]
+        - jnp.abs(after) * product[:, y_size : 2 * y_size]
+        - before * product[:, 2 * y_size : 3 * y_size]
+        + jnp.abs(before) * product[:, 3 * y_size :]
+    )
+
     def one(t, carry):
-        def load(x, at):
-            if first:
-                return section[pl.ds(pl.multiple_of(t * 8 * x_size, 8 * x_size) + x, 8, stride=x_size), :]
-            return section[x, at, :]
-
-        def base(x):
-            return base_ref[pl.ds(pl.multiple_of(t * 8 * x_size, 8 * x_size) + x, 8, stride=x_size), :]
-
-        def store(x, at, new):
-            if last:
-                out[pl.ds(pl.multiple_of(t * 8 * x_size, 8 * x_size) + x, 8, stride=x_size), :] = new
-                return
-            out[x, at, :] = new
-            if x < WIDTH:
-                low[x, at, :] = new
-            if x >= x_size - WIDTH:
-                high[x - x_size + WIDTH, at, :] = new
-
-        edges = section_tile(
-            t, x_size, divisor, load, base, (west, east), (south, north, own), (speed_x, speed_y, speed_edge), factor, store
-        )
+        at = pl.ds(pl.multiple_of(t * 8, 8), 8)
+        start = pl.multiple_of(t * 8 * x_size, 8 * x_size)
+
+        def across(ref, x):
+            return ref[pl.ds(start + x, 8, stride=x_size), :]
+
+        def cell(x):
+            if x < 0:
+                return west[x + WIDTH][at, :]
+            if x >= x_size:
+                return east[x - x_size][at, :]
+            return across(section, x) if first else section[x, at, :]
+
+        lane = lane_index((8, y_size))
+        edge_lane = (lane < WIDTH) | (lane >= y_size - WIDTH)
+        edge_share = share[at, :]
+        q = [cell(x) for x in range(-3, 2)]
+        d1 = [q[i + 1] - q[i] for i in range(4)]
+        d2 = [d1[i + 1] - d1[i] for i in range(3)]
+        d3 = [d2[i + 1] - d2[i] for i in range(2)]
+        d4 = d3[1] - d3[0]
+        smooth = d4 - 5.0 * d2[1] + 30.0 * q[2]
+        q, d1, d2, d3 = q[3:], d1[-1], d2[-1], d3[-1]
+        flux_before = None
+        edges = None
+        for x in range(-1, x_size):
+            q.append(cell(x + WIDTH))
+            new1 = q[-1] - q[-2]
+            new2 = new1 - d1
+            new3 = new2 - d2
+            new4 = new3 - d3
+            new_smooth = new4 - 5.0 * d2 + 30.0 * q[0]
+            speed = speed_x[x + 1, at, :]
+            flux = speed * (smooth + new_smooth) - jnp.abs(speed) * (new4 - d4)
+            d1, d2, d3, d4, smooth = new1, new2, new3, new4, new_smooth
+            if x >= 0:
+                if first:
+                    lines = [across(part, x) for part in parts]
+                else:
+                    lines = [part[pl.ds(pl.multiple_of(x * rows + t * 8, 8), 8), :] for part in parts]
+                after, before = ahead_y[x, at, :], behind_y[x, at, :]
+                moved = rolled(edge_share, -(GROUP * x + WIDTH))
+                divergence = (
+                    (flux - flux_before)
+                    + (after * lines[0] - jnp.abs(after) * lines[1])
+                    - (before * lines[2] - jnp.abs(before) * lines[3])
+                    + jnp.where(edge_lane, moved, 0.0)
+                )
+                new = across(base_ref, x) + scales[k, x] * divergence
+                if last:
+                    out[pl.ds(start + x, 8, stride=x_size), :] = new
+                else:
+                    out[x, at, :] = new
+                    if x < WIDTH:
+                        low[x, at, :] = new
+                    if x >= x_size - WIDTH:
+                        high[x - x_size + WIDTH, at, :] = new
+                    edges = pack_edges(edges, new, x)
+            flux_before = flux
+            q = q[1:]
         if not last:
-            packed[pl.ds(pl.multiple_of(t * 8, 8), 8), :] = edges
+            packed[at, :] = edges
         return carry
 
     lax.fori_loop(0, rows // 8, one, 0)
@@ -333,12 +373,20 @@
     speeds = pl.pallas_call(
         functools.partial(wind_kernel, x_size),
         grid=(1,),
-        in_specs=[whole, edge_row, edge_row, edge_pack, edge_pack, edge_pack],
-        out_specs=[whole] * 3,
-        out_shape=[f32((x_size + 1, levels, y_size)), f32((x_size, levels, y_size)), f32((levels, y_size))],
+        in_specs=[whole, whole, edge_row, edge_row, edge_pack, edge_pack],
+        out_specs=[whole] * 6,
+        out_shape=[
+            f32((x_size + 1, levels, y_size)),
+            f32((x_size, levels, y_size)),
+            f32((x_size, levels, y_size)),
+            f32((levels, y_size)),
+            f32((levels, y_size)),
+            f32((len(DIVISORS), x_size, 8, y_size)),
+        ],
         compiler_params=params,
         name="speeds",
-    )(wind, west, east, south, north, packs[0])
+    )(wind, map_factor, west, east, south, north)
+    matrices = stencil_matrices(y_size)
 
     block = levels
     steps = rows // block
@@ -351,8 +399,8 @@
     cost = pl.CostEstimate(flops=flops, bytes_accessed=16 * rows * x_size * y_size, transcendentals=0)
     sections = [None] * CHUNKS
     result = None
-    for k, divisor in enumerate((3.0, 2.0, 1.0)):
-        last = k == 2
+    for k in range(len(DIVISORS)):
+        last = k == len(DIVISORS) - 1
         for c in range(CHUNKS):
             west, east, south, north = received[c]
             flat_c = pl.BlockSpec((block * x_size, y_size), lambda g, c=c: (c * steps + g, 0))
@@ -360,8 +408,8 @@
             specs = [flat_c] if k == 0 else [tall, flat_c]
             operands += [west.reshape(-1, y_size)] * 3 + [east.reshape(-1, y_size)] * 3
             specs += row_specs * 2
-            operands += [south, north, packs[c], *speeds, map_factor]
-            specs += [pack] * 3 + [whole] * 4
+            operands += [south, north, *speeds, *matrices]
+            specs += [pack] * 2 + [whole] * 8
             city = last and c == 0
             aliases = {}
             if city:
@@ -391,11 +439,13 @@
                     f32((rows, y_size)),
                 ]
             outs = pl.pallas_call(
-                functools.partial(section_kernel, x_size, divisor, k == 0, last, city),
+                functools.partial(section_kernel, x_size, k, last, city),
                 grid=(steps,),
                 in_specs=specs,
                 out_specs=out_specs,
                 out_shape=out_shape,
+                scratch_shapes=[pltpu.VMEM((block, y_size), jnp.float32)]
+                + [pltpu.VMEM((block * x_size, y_size), jnp.float32)] * 4,
                 input_output_aliases=aliases,
                 compiler_params=params,
                 cost_estimate=cost,

time: 89.9 us -> 78.9 us (0.88)
  Pallas kernels: 42.7 us -> 31.7 us
    pallas_call x6, Pallas kernels: 37.8 us -> 26.2 us  [per_device(): pl.pallas_call(functools.partial(section_kernel, x_size, k, last, city),...]
    unnamed x20 -> x24, local copies, waits for them, and re-layouts: 2.86 us -> 2.87 us
  transfers between devices with their start and end apart: 24 -> 24, of which waited for: 4 -> 4; matrix products, arithmetic and copies ran while one was open for 0% -> 0% of each run, Pallas kernels for 38% -> 33%
where the time goes in v2:
time: 78.9 us; the launch traced here: 78.6 us
  Pallas kernels  31.7 us (40%)
  starting transfers between devices  29.7 us (38%)
  waiting for transfers between devices  12.8 us (16%)
  local copies, waits for them, and re-layouts  2.87 us (4%)
  between operations  1.55 us (2%)
    ppermute x24, starting transfers between devices, exchange(): return (lax.ppermute(high, axis, up), lax.ppermute(low, axis, down))  29.7 us
    pallas_call x6, Pallas kernels, per_device(): pl.pallas_call(functools.partial(section_kernel, x_size, k, last, city),...  26.2 us
    ppermute x24, waiting for transfers between devices, exchange(): return (lax.ppermute(high, axis, up), lax.ppermute(low, axis, down))  12.8 us
    pallas_call x2, Pallas kernels, per_device(): pl.pallas_call(functools.partial(extract_kernel, None, x_size, c == 0), g...  3.62 us
    unnamed x24, local copies, waits for them, and re-layouts  2.87 us
    pallas_call x1, Pallas kernels, per_device(): pl.pallas_call(functools.partial(wind_kernel, x_size), grid=(1,), in_spec...  1.95 us
  transfers between devices with their start and end apart: 24, of which 4 were waited for; matrix products, arithmetic and copies ran while one was open for 0% of the time, Pallas kernels for 33%

profile of v2, /device:TPU:0, one launch (start us, length us, event | category | flops | bytes accessed | tf_op | source)
XLA Modules:
  0.0 78.6 jit_solution(3716240798649947390)
XLA Ops:
  0.6 1.6 %copy-done = f32[4,64,16,128]{3,2,1,0:T(8,128)S(1)} copy-done((f32[4,64,16,128]{3,2,1,0:T(8,128)S(1)}, f32[4,64,16,128]{3,2,1,0:T(8,128)}, u32[]{:S(2)}) %copy-start) | copy-done | bytes 2097176
  2.2 1.2 %copy-done.4 = f32[2,64,16,128]{3,2,1,0:T(8,128)S(1)} copy-done((f32[2,64,16,128]{3,2,1,0:T(8,128)S(1)}, f32[2,64,16,128]{3,2,1,0:T(8,128)}, u32[]{:S(2)}) %copy-start.4) | copy-done | bytes 1048600
  3.5 2.2 %extract.3 = (f32[448,128]{1,0:T(8,128)S(1)}, f32[448,128]{1,0:T(8,128)S(1)}, f32[192,128]{1,0:T(8,128)S(1)}) custom-call(f32[4096,128]{1,0:T(8,128)S(1)} %bitcast.15, f32[2048,128]{1,0:T(8,128)S(1)} %bitcast.23), custom_call_target="tpu_custom_call" | custom-call | tf_op jit(solution)/shard_map/extract/pallas_call | solution.py:350
  5.7 3.1 %collective-permute-start.4 = (f32[448,128]{1,0:T(8,128)S(1)}, f32[448,128]{1,0:T(8,128)S(1)}, u32[]{:S(2)}, u32[]{:S(2)}) collective-permute-start(f32[448,128]{1,0:T(8,128)S(1)} %get-tuple-element.37), channel_id=1, source_target_pairs={{0,8},{8,16},{16,24},{24,0},{1,9},{9,17},{17,25},{25,1},{2,10},{10... | collective-permute-start | bytes 688136 | tf_op jit(solution)/shard_map/ppermute | solution.py:324
  8.8 2.1 %collective-permute-start.5 = (f32[448,128]{1,0:T(8,128)S(1)}, f32[448,128]{1,0:T(8,128)S(1)}, u32[]{:S(2)}, u32[]{:S(2)}) collective-permute-start(f32[448,128]{1,0:T(8,128)S(1)} %get-tuple-element.38), channel_id=1, source_target_pairs={{8,0},{16,8},{24,16},{0,24},{9,1},{17,9},{25,17},{1,25},{10,2},{18... | collective-permute-start | bytes 688136 | tf_op jit(solution)/shard_map/ppermute | solution.py:324
  10.8 1.6 %collective-permute-start.7 = (f32[192,128]{1,0:T(8,128)S(1)}, f32[192,128]{1,0:T(8,128)S(1)}, u32[]{:S(2)}, u32[]{:S(2)}) collective-permute-start(f32[192,128]{1,0:T(8,128)S(1)} %get-tuple-element.39), channel_id=1, source_target_pairs={{1,0},{2,1},{3,2},{4,3},{5,4},{6,5},{7,6},{0,7},{9,8},{10,9},{11,1... | collective-permute-start | bytes 294920 | tf_op jit(solution)/shard_map/ppermute | solution.py:324
  12.5 1.4 %extract.2 = (f32[384,128]{1,0:T(8,128)S(1)}, f32[384,128]{1,0:T(8,128)S(1)}, f32[128,128]{1,0:T(8,128)S(1)}) custom-call(f32[4096,128]{1,0:T(8,128)S(1)} %bitcast.16), custom_call_target="tpu_custom_call" | custom-call | tf_op jit(solution)/shard_map/extract/pallas_call | solution.py:350
  13.9 0.1 collective-permute-start
  14.0 1.1 %collective-permute-done.7.north.refs_8_ = f32[192,128]{1,0:T(8,128)S(1)} collective-permute-done((f32[192,128]{1,0:T(8,128)S(1)}, f32[192,128]{1,0:T(8,128)S(1)}, u32[]{:S(2)}, u32[]{:S(2)}) %collective-permute-start.7) | collective-permute-done | bytes 98336 | tf_op jit(solution)/shard_map/ppermute | solution.py:324
  15.1 2.7 %collective-permute-start.1 = (f32[384,128]{1,0:T(8,128)S(1)}, f32[384,128]{1,0:T(8,128)S(1)}, u32[]{:S(2)}, u32[]{:S(2)}) collective-permute-start(f32[384,128]{1,0:T(8,128)S(1)} %get-tuple-element.35), channel_id=1, source_target_pairs={{8,0},{16,8},{24,16},{0,24},{9,1},{17,9},{25,17},{1,25},{10,2},{18... | collective-permute-start | bytes 589832 | tf_op jit(solution)/shard_map/ppermute | solution.py:324
  17.8 2.1 %collective-permute-start.3 = (f32[128,128]{1,0:T(8,128)S(1)}, f32[128,128]{1,0:T(8,128)S(1)}, u32[]{:S(2)}, u32[]{:S(2)}) collective-permute-start(f32[128,128]{1,0:T(8,128)S(1)} %get-tuple-element.36), channel_id=1, source_target_pairs={{1,0},{2,1},{3,2},{4,3},{5,4},{6,5},{7,6},{0,7},{9,8},{10,9},{11,1... | collective-permute-start | bytes 196616 | tf_op jit(solution)/shard_map/ppermute | solution.py:324
  19.9 2.4 %collective-permute-done.5.east.refs_4_.refs_5_.refs_6_ = f32[448,128]{1,0:T(8,128)S(1)} collective-permute-done((f32[448,128]{1,0:T(8,128)S(1)}, f32[448,128]{1,0:T(8,128)S(1)}, u32[]{:S(2)}, u32[]{:S(2)}) %collective-permute-start.5) | collective-permute-done | bytes 229408 | tf_op jit(solution)/shard_map/ppermute | solution.py:324
  22.3 2.0 %speeds.1 = (f32[17,64,128]{2,1,0:T(8,128)S(1)}, f32[16,64,128]{2,1,0:T(8,128)S(1)}, f32[16,64,128]{2,1,0:T(8,128)S(1)}, f32[64,128]{1,0:T(8,128)S(1)}, f32[64,1...) custom-call(f32[2048,128]{1,0:T(8,128)S(1)} %bitcast.24, f32[16,128]{1,0:T(8,128)S(1)} %copy-done.7, ...), custom_call_target="tpu_custom_call" | custom-call | tf_op jit(solution)/shard_map/speeds/pallas_call | solution.py:373
  24.3 4.6 %section_0_0.1 = (f32[16,128,128]{2,1,0:T(8,128)S(1)}, f32[3,128,128]{2,1,0:T(8,128)S(1)}, f32[3,128,128]{2,1,0:T(8,128)S(1)}, f32[128,128]{1,0:T(8,128)S(1)}) custom-call(f32[4096,128]{1,0:T(8,128)S(1)} %bitcast.17, f32[448,128]{1,0:T(8,128)S(1)} %collective-permute-done.4.west.refs_1_.refs_2_.refs_3_, ...), custom_call_target="tpu_custom_call" | custom-call | flops 35389440 | bytes 4194304 | tf_op jit(solution)/shard_map/section_0_0/pallas_call | solution.py:441
  29.0 0.5 collective-permute-start.16
  29.5 3.4 %collective-permute-start.17 = (f32[3,128,128]{2,1,0:T(8,128)S(1)}, f32[3,128,128]{2,1,0:T(8,128)S(1)}, u32[]{:S(2)}, u32[]{:S(2)}) collective-permute-start(f32[3,128,128]{2,1,0:T(8,128)S(1)} %get-tuple-element.56), channel_id=1, source_target_pairs={{8,0},{16,8},{24,16},{0,24},{9,1},{17,9},{25,17},{1,25},{10,2},{18... | collective-permute-start | bytes 589832 | tf_op jit(solution)/shard_map/ppermute | solution.py:324
  32.9 4.6 %section_0_1.1 = (f32[16,128,128]{2,1,0:T(8,128)S(1)}, f32[3,128,128]{2,1,0:T(8,128)S(1)}, f32[3,128,128]{2,1,0:T(8,128)S(1)}, f32[128,128]{1,0:T(8,128)S(1)}) custom-call(f32[4096,128]{1,0:T(8,128)S(1)} %bitcast.18, f32[384,128]{1,0:T(8,128)S(1)} %collective-permute-done.refs_1_.refs_2_.refs_3_, ...), custom_call_target="tpu_custom_call" | custom-call | flops 35389440 | bytes 4194304 | tf_op jit(solution)/shard_map/section_0_1/pallas_call | solution.py:441
  37.5 0.2 collective-permute-start.8
  37.7 3.7 %collective-permute-start.9 = (f32[3,128,128]{2,1,0:T(8,128)S(1)}, f32[3,128,128]{2,1,0:T(8,128)S(1)}, u32[]{:S(2)}, u32[]{:S(2)}) collective-permute-start(f32[3,128,128]{2,1,0:T(8,128)S(1)} %get-tuple-element.48), channel_id=1, source_target_pairs={{8,0},{16,8},{24,16},{0,24},{9,1},{17,9},{25,17},{1,25},{10,2},{18... | collective-permute-start | bytes 589832 | tf_op jit(solution)/shard_map/ppermute | solution.py:324
  41.4 4.6 %collective-permute-done.18.refs_8_ = f32[128,128]{1,0:T(8,128)S(1)} collective-permute-done((f32[128,128]{1,0:T(8,128)S(1)}, f32[128,128]{1,0:T(8,128)S(1)}, u32[]{:S(2)}, u32[]{:S(2)}) %collective-permute-start.18) | collective-permute-done | bytes 65568 | tf_op jit(solution)/shard_map/ppermute | solution.py:324
  46.0 0.5 collective-permute-start.10
  46.5 4.1 %section_1_0.1 = (f32[16,128,128]{2,1,0:T(8,128)S(1)}, f32[3,128,128]{2,1,0:T(8,128)S(1)}, f32[3,128,128]{2,1,0:T(8,128)S(1)}, f32[128,128]{1,0:T(8,128)S(1)}) custom-call(f32[16,128,128]{2,1,0:T(8,128)S(1)} %get-tuple-element.54.refs_0_, f32[4096,128]{1,0:T(8,128)S(1)} %bitcast.19, f32[384,128]{1,0:T(8,128)S(1)} %bitcast.34, f32[384,128]{1,0:T(8,128)S(1)} %bitcast.35, ...), custom_call_target="tpu_custom_call" | custom-call | flops 35389440 | bytes 4194304 | tf_op jit(solution)/shard_map/section_1_0/pallas_call | solution.py:441
  50.6 0.1 collective-permute-start.20
  50.7 3.8 %collective-permute-start.21 = (f32[3,128,128]{2,1,0:T(8,128)S(1)}, f32[3,128,128]{2,1,0:T(8,128)S(1)}, u32[]{:S(2)}, u32[]{:S(2)}) collective-permute-start(f32[3,128,128]{2,1,0:T(8,128)S(1)} %get-tuple-element.60), channel_id=1, source_target_pairs={{8,0},{16,8},{24,16},{0,24},{9,1},{17,9},{25,17},{1,25},{10,2},{18... | collective-permute-start | bytes 589832 | tf_op jit(solution)/shard_map/ppermute | solution.py:324
  54.5 1.6 %collective-permute-start.23 = (f32[128,128]{1,0:T(8,128)S(1)}, f32[128,128]{1,0:T(8,128)S(1)}, u32[]{:S(2)}, u32[]{:S(2)}) collective-permute-start(f32[128,128]{1,0:T(8,128)S(1)} %get-tuple-element.61), channel_id=1, source_target_pairs={{1,0},{2,1},{3,2},{4,3},{5,4},{6,5},{7,6},{0,7},{9,8},{10,9},{11,1... | collective-permute-start | bytes 196616 | tf_op jit(solution)/shard_map/ppermute | solution.py:324
  56.1 4.1 %section_1_1.1 = (f32[16,128,128]{2,1,0:T(8,128)S(1)}, f32[3,128,128]{2,1,0:T(8,128)S(1)}, f32[3,128,128]{2,1,0:T(8,128)S(1)}, f32[128,128]{1,0:T(8,128)S(1)}) custom-call(f32[16,128,128]{2,1,0:T(8,128)S(1)} %get-tuple-element.46.refs_0_, f32[4096,128]{1,0:T(8,128)S(1)} %bitcast.20, f32[384,128]{1,0:T(8,128)S(1)} %bitcast.31, f32[384,128]{1,0:T(8,128)S(1)} %bitcast.32, ...), custom_call_target="tpu_custom_call" | custom-call | flops 35389440 | bytes 4194304 | tf_op jit(solution)/shard_map/section_1_1/pallas_call | solution.py:441
  60.3 0.1 collective-permute-start.12
  60.3 3.8 %collective-permute-start.13 = (f32[3,128,128]{2,1,0:T(8,128)S(1)}, f32[3,128,128]{2,1,0:T(8,128)S(1)}, u32[]{:S(2)}, u32[]{:S(2)}) collective-permute-start(f32[3,128,128]{2,1,0:T(8,128)S(1)} %get-tuple-element.52), channel_id=1, source_target_pairs={{8,0},{16,8},{24,16},{0,24},{9,1},{17,9},{25,17},{1,25},{10,2},{18... | collective-permute-start | bytes 589832 | tf_op jit(solution)/shard_map/ppermute | solution.py:324
  64.2 4.6 %collective-permute-done.22.refs_8_ = f32[128,128]{1,0:T(8,128)S(1)} collective-permute-done((f32[128,128]{1,0:T(8,128)S(1)}, f32[128,128]{1,0:T(8,128)S(1)}, u32[]{:S(2)}, u32[]{:S(2)}) %collective-permute-start.22) | collective-permute-done | bytes 65568 | tf_op jit(solution)/shard_map/ppermute | solution.py:324
  68.8 0.5 collective-permute-start.14
  70.0 4.9 %section_2_0.1 = (f32[4096,128]{1,0:T(8,128)}, f32[10,256]{1,0:T(8,128)}, f32[1,256]{1,0:T(1,128)}) custom-call(f32[16,128,128]{2,1,0:T(8,128)S(1)} %get-tuple-element.58.refs_0_, f32[4096,128]{1,0:T(8,128)S(1)} %bitcast.21, f32[384,128]{1,0:T(8,128)S(1)} %bitcast.25, f32[384,128]{1,0:T(8,128)S(1)} %bitcast.26, f32[384,128]{1,0:T(8,128)S(1)} %bitcast.27, ...), custom_call_target="tpu_custom_call" | custom-call | flops 35389440 | bytes 4194304 | tf_op jit(solution)/shard_map/section_2_0/pallas_call | solution.py:441
  74.9 3.8 %section_2_1.1 = f32[4096,128]{1,0:T(8,128)} custom-call(f32[16,128,128]{2,1,0:T(8,128)S(1)} %get-tuple-element.50.refs_0_, f32[4096,128]{1,0:T(8,128)S(1)} %bitcast.22, f32[384,128]{1,0:T(8,128)S(1)} %bitcast.40, f32[384,128]{1,0:T(8,128)S(1)} %bitcast.41, f32[384,128]{1,0:T(8,128)S(1)} %bitcast.42, ...), custom_call_target="tpu_custom_call", output_to_operand_aliasing={{}: (18, {})} | custom-call | flops 35389440 | bytes 4194304 | tf_op jit(solution)/shard_map/section_2_1/pallas_call | solution.py:441
  (49 shorter events, 0.1 us)
Async XLA Ops:
  3.5 18.9 %copy-start.5 = (f32[2,64,16,128]{3,2,1,0:T(8,128)S(1)}, f32[2,64,16,128]{3,2,1,0:T(8,128)}, u32[]{:S(2)}) copy-start(f32[2,64,16,128]{3,2,1,0:T(8,128)} %param.12) | copy-start | bytes 3145732
  3.5 18.9 %copy-start.7 = (f32[16,128]{1,0:T(8,128)S(1)}, f32[16,128]{1,0:T(8,128)}, u32[]{:S(2)}) copy-start(f32[16,128]{1,0:T(8,128)} %factor.1) | copy-start | bytes 24580
  5.6 18.7 %copy-start.1 = (f32[4,64,16,128]{3,2,1,0:T(8,128)S(1)}, f32[4,64,16,128]{3,2,1,0:T(8,128)}, u32[]{:S(2)}) copy-start(f32[4,64,16,128]{3,2,1,0:T(8,128)} %param.11) | copy-start | bytes 6291460
  5.7 18.6 %copy-start.2 = (bf16[256,512]{1,0:T(8,128)(2,1)S(1)}, bf16[256,512]{1,0:T(8,128)(2,1)}, u32[]{:S(2)}) copy-start(bf16[256,512]{1,0:T(8,128)(2,1)} %constant.5.clone.refs_16_.refs_17_) | copy-start | bytes 786436
  5.7 18.6 %copy-start.3 = (bf16[256,512]{1,0:T(8,128)(2,1)S(1)}, bf16[256,512]{1,0:T(8,128)(2,1)}, u32[]{:S(2)}) copy-start(bf16[256,512]{1,0:T(8,128)(2,1)} %constant.4.clone.refs_15_.refs_16_) | copy-start | bytes 786436
  5.7 14.2 %collective-permute-start.4 = (f32[448,128]{1,0:T(8,128)S(1)}, f32[448,128]{1,0:T(8,128)S(1)}, u32[]{:S(2)}, u32[]{:S(2)}) collective-permute-start(f32[448,128]{1,0:T(8,128)S(1)} %get-tuple-element.37), channel_id=1, source_target_pairs={{0,8},{8,16},{16,24},{24,0},{1,9},{9,17},{17,25},{25,1},{2,10},{10... | collective-permute-start | bytes 688136 | tf_op jit(solution)/shard_map/ppermute | solution.py:324
  8.8 13.6 %collective-permute-start.5 = (f32[448,128]{1,0:T(8,128)S(1)}, f32[448,128]{1,0:T(8,128)S(1)}, u32[]{:S(2)}, u32[]{:S(2)}) collective-permute-start(f32[448,128]{1,0:T(8,128)S(1)} %get-tuple-element.38), channel_id=1, source_target_pairs={{8,0},{16,8},{24,16},{0,24},{9,1},{17,9},{25,17},{1,25},{10,2},{18... | collective-permute-start | bytes 688136 | tf_op jit(solution)/shard_map/ppermute | solution.py:324
  10.8 4.3 %collective-permute-start.7 = (f32[192,128]{1,0:T(8,128)S(1)}, f32[192,128]{1,0:T(8,128)S(1)}, u32[]{:S(2)}, u32[]{:S(2)}) collective-permute-start(f32[192,128]{1,0:T(8,128)S(1)} %get-tuple-element.39), channel_id=1, source_target_pairs={{1,0},{2,1},{3,2},{4,3},{5,4},{6,5},{7,6},{0,7},{9,8},{10,9},{11,1... | collective-permute-start | bytes 294920 | tf_op jit(solution)/shard_map/ppermute | solution.py:324
  12.5 5.3 %collective-permute-start.6 = (f32[192,128]{1,0:T(8,128)S(1)}, f32[192,128]{1,0:T(8,128)S(1)}, u32[]{:S(2)}, u32[]{:S(2)}) collective-permute-start(f32[192,128]{1,0:T(8,128)S(1)} %get-tuple-element.39), channel_id=1, source_target_pairs={{0,1},{1,2},{2,3},{3,4},{4,5},{5,6},{6,7},{7,0},{8,9},{9,10},{10,1... | collective-permute-start | bytes 294920 | tf_op jit(solution)/shard_map/ppermute | solution.py:324
  13.9 19.0 %collective-permute-start = (f32[384,128]{1,0:T(8,128)S(1)}, f32[384,128]{1,0:T(8,128)S(1)}, u32[]{:S(2)}, u32[]{:S(2)}) collective-permute-start(f32[384,128]{1,0:T(8,128)S(1)} %get-tuple-element.34), channel_id=1, source_target_pairs={{0,8},{8,16},{16,24},{24,0},{1,9},{9,17},{17,25},{25,1},{2,10},{10... | collective-permute-start | bytes 589832 | tf_op jit(solution)/shard_map/ppermute | solution.py:324
  15.1 17.8 %collective-permute-start.1 = (f32[384,128]{1,0:T(8,128)S(1)}, f32[384,128]{1,0:T(8,128)S(1)}, u32[]{:S(2)}, u32[]{:S(2)}) collective-permute-start(f32[384,128]{1,0:T(8,128)S(1)} %get-tuple-element.35), channel_id=1, source_target_pairs={{8,0},{16,8},{24,16},{0,24},{9,1},{17,9},{25,17},{1,25},{10,2},{18... | collective-permute-start | bytes 589832 | tf_op jit(solution)/shard_map/ppermute | solution.py:324
  17.8 11.7 %collective-permute-start.3 = (f32[128,128]{1,0:T(8,128)S(1)}, f32[128,128]{1,0:T(8,128)S(1)}, u32[]{:S(2)}, u32[]{:S(2)}) collective-permute-start(f32[128,128]{1,0:T(8,128)S(1)} %get-tuple-element.36), channel_id=1, source_target_pairs={{1,0},{2,1},{3,2},{4,3},{5,4},{6,5},{7,6},{0,7},{9,8},{10,9},{11,1... | collective-permute-start | bytes 196616 | tf_op jit(solution)/shard_map/ppermute | solution.py:324
  19.9 13.0 %collective-permute-start.2 = (f32[128,128]{1,0:T(8,128)S(1)}, f32[128,128]{1,0:T(8,128)S(1)}, u32[]{:S(2)}, u32[]{:S(2)}) collective-permute-start(f32[128,128]{1,0:T(8,128)S(1)} %get-tuple-element.36), channel_id=1, source_target_pairs={{0,1},{1,2},{2,3},{3,4},{4,5},{5,6},{6,7},{7,0},{8,9},{9,10},{10,1... | collective-permute-start | bytes 196616 | tf_op jit(solution)/shard_map/ppermute | solution.py:324
  29.0 17.0 %collective-permute-start.16 = (f32[3,128,128]{2,1,0:T(8,128)S(1)}, f32[3,128,128]{2,1,0:T(8,128)S(1)}, u32[]{:S(2)}, u32[]{:S(2)}) collective-permute-start(f32[3,128,128]{2,1,0:T(8,128)S(1)} %get-tuple-element.55), channel_id=1, source_target_pairs={{0,8},{8,16},{16,24},{24,0},{1,9},{9,17},{17,25},{25,1},{2,10},{10... | collective-permute-start | bytes 589832 | tf_op jit(solution)/shard_map/ppermute | solution.py:324
  29.5 17.0 %collective-permute-start.17 = (f32[3,128,128]{2,1,0:T(8,128)S(1)}, f32[3,128,128]{2,1,0:T(8,128)S(1)}, u32[]{:S(2)}, u32[]{:S(2)}) collective-permute-start(f32[3,128,128]{2,1,0:T(8,128)S(1)} %get-tuple-element.56), channel_id=1, source_target_pairs={{8,0},{16,8},{24,16},{0,24},{9,1},{17,9},{25,17},{1,25},{10,2},{18... | collective-permute-start | bytes 589832 | tf_op jit(solution)/shard_map/ppermute | solution.py:324
  32.9 8.6 %collective-permute-start.19 = (f32[128,128]{1,0:T(8,128)S(1)}, f32[128,128]{1,0:T(8,128)S(1)}, u32[]{:S(2)}, u32[]{:S(2)}) collective-permute-start(f32[128,128]{1,0:T(8,128)S(1)} %get-tuple-element.57), channel_id=1, source_target_pairs={{1,0},{2,1},{3,2},{4,3},{5,4},{6,5},{7,6},{0,7},{9,8},{10,9},{11,1... | collective-permute-start | bytes 196616 | tf_op jit(solution)/shard_map/ppermute | solution.py:324
  37.5 18.6 %collective-permute-start.8 = (f32[3,128,128]{2,1,0:T(8,128)S(1)}, f32[3,128,128]{2,1,0:T(8,128)S(1)}, u32[]{:S(2)}, u32[]{:S(2)}) collective-permute-start(f32[3,128,128]{2,1,0:T(8,128)S(1)} %get-tuple-element.47), channel_id=1, source_target_pairs={{0,8},{8,16},{16,24},{24,0},{1,9},{9,17},{17,25},{25,1},{2,10},{10... | collective-permute-start | bytes 589832 | tf_op jit(solution)/shard_map/ppermute | solution.py:324
  37.7 18.4 %collective-permute-start.9 = (f32[3,128,128]{2,1,0:T(8,128)S(1)}, f32[3,128,128]{2,1,0:T(8,128)S(1)}, u32[]{:S(2)}, u32[]{:S(2)}) collective-permute-start(f32[3,128,128]{2,1,0:T(8,128)S(1)} %get-tuple-element.48), channel_id=1, source_target_pairs={{8,0},{16,8},{24,16},{0,24},{9,1},{17,9},{25,17},{1,25},{10,2},{18... | collective-permute-start | bytes 589832 | tf_op jit(solution)/shard_map/ppermute | solution.py:324
  41.4 4.6 %collective-permute-start.18 = (f32[128,128]{1,0:T(8,128)S(1)}, f32[128,128]{1,0:T(8,128)S(1)}, u32[]{:S(2)}, u32[]{:S(2)}) collective-permute-start(f32[128,128]{1,0:T(8,128)S(1)} %get-tuple-element.57), channel_id=1, source_target_pairs={{0,1},{1,2},{2,3},{3,4},{4,5},{5,6},{6,7},{7,0},{8,9},{9,10},{10,1... | collective-permute-start | bytes 196616 | tf_op jit(solution)/shard_map/ppermute | solution.py:324
  46.0 4.7 %collective-permute-start.11 = (f32[128,128]{1,0:T(8,128)S(1)}, f32[128,128]{1,0:T(8,128)S(1)}, u32[]{:S(2)}, u32[]{:S(2)}) collective-permute-start(f32[128,128]{1,0:T(8,128)S(1)} %get-tuple-element.49), channel_id=1, source_target_pairs={{1,0},{2,1},{3,2},{4,3},{5,4},{6,5},{7,6},{0,7},{9,8},{10,9},{11,1... | collective-permute-start | bytes 196616 | tf_op jit(solution)/shard_map/ppermute | solution.py:324
  46.0 8.5 %collective-permute-start.10 = (f32[128,128]{1,0:T(8,128)S(1)}, f32[128,128]{1,0:T(8,128)S(1)}, u32[]{:S(2)}, u32[]{:S(2)}) collective-permute-start(f32[128,128]{1,0:T(8,128)S(1)} %get-tuple-element.49), channel_id=1, source_target_pairs={{0,1},{1,2},{2,3},{3,4},{4,5},{5,6},{6,7},{7,0},{8,9},{9,10},{10,1... | collective-permute-start | bytes 196616 | tf_op jit(solution)/shard_map/ppermute | solution.py:324
  50.6 18.1 %collective-permute-start.20 = (f32[3,128,128]{2,1,0:T(8,128)S(1)}, f32[3,128,128]{2,1,0:T(8,128)S(1)}, u32[]{:S(2)}, u32[]{:S(2)}) collective-permute-start(f32[3,128,128]{2,1,0:T(8,128)S(1)} %get-tuple-element.59), channel_id=1, source_target_pairs={{0,8},{8,16},{16,24},{24,0},{1,9},{9,17},{17,25},{25,1},{2,10},{10... | collective-permute-start | bytes 589832 | tf_op jit(solution)/shard_map/ppermute | solution.py:324
  50.7 19.2 %collective-permute-start.21 = (f32[3,128,128]{2,1,0:T(8,128)S(1)}, f32[3,128,128]{2,1,0:T(8,128)S(1)}, u32[]{:S(2)}, u32[]{:S(2)}) collective-permute-start(f32[3,128,128]{2,1,0:T(8,128)S(1)} %get-tuple-element.60), channel_id=1, source_target_pairs={{8,0},{16,8},{24,16},{0,24},{9,1},{17,9},{25,17},{1,25},{10,2},{18... | collective-permute-start | bytes 589832 | tf_op jit(solution)/shard_map/ppermute | solution.py:324
  54.5 9.7 %collective-permute-start.23 = (f32[128,128]{1,0:T(8,128)S(1)}, f32[128,128]{1,0:T(8,128)S(1)}, u32[]{:S(2)}, u32[]{:S(2)}) collective-permute-start(f32[128,128]{1,0:T(8,128)S(1)} %get-tuple-element.61), channel_id=1, source_target_pairs={{1,0},{2,1},{3,2},{4,3},{5,4},{6,5},{7,6},{0,7},{9,8},{10,9},{11,1... | collective-permute-start | bytes 196616 | tf_op jit(solution)/shard_map/ppermute | solution.py:324
  56.1 13.8 %copy-start.8 = (f32[10,10]{1,0:T(8,128)S(1)}, f32[10,10]{1,0:T(8,128)}, u32[]{:S(2)}) copy-start(f32[10,10]{1,0:T(8,128)} %refs_21_.1) | copy-start | bytes 1204
  56.1 13.8 %copy-start.9 = (s32[256]{0:T(256)S(1)}, s32[256]{0:T(256)}, u32[]{:S(2)}) copy-start(s32[256]{0:T(256)} %param.15) | copy-start | bytes 3076
  56.1 13.8 %copy-start.10 = (s32[256]{0:T(256)S(1)}, s32[256]{0:T(256)}, u32[]{:S(2)}) copy-start(s32[256]{0:T(256)} %param.16) | copy-start | bytes 3076
  60.3 14.6 %collective-permute-start.12 = (f32[3,128,128]{2,1,0:T(8,128)S(1)}, f32[3,128,128]{2,1,0:T(8,128)S(1)}, u32[]{:S(2)}, u32[]{:S(2)}) collective-permute-start(f32[3,128,128]{2,1,0:T(8,128)S(1)} %get-tuple-element.51), channel_id=1, source_target_pairs={{0,8},{8,16},{16,24},{24,0},{1,9},{9,17},{17,25},{25,1},{2,10},{10... | collective-permute-start | bytes 589832 | tf_op jit(solution)/shard_map/ppermute | solution.py:324
  60.3 14.5 %collective-permute-start.13 = (f32[3,128,128]{2,1,0:T(8,128)S(1)}, f32[3,128,128]{2,1,0:T(8,128)S(1)}, u32[]{:S(2)}, u32[]{:S(2)}) collective-permute-start(f32[3,128,128]{2,1,0:T(8,128)S(1)} %get-tuple-element.52), channel_id=1, source_target_pairs={{8,0},{16,8},{24,16},{0,24},{9,1},{17,9},{25,17},{1,25},{10,2},{18... | collective-permute-start | bytes 589832 | tf_op jit(solution)/shard_map/ppermute | solution.py:324
  64.2 4.6 %collective-permute-start.22 = (f32[128,128]{1,0:T(8,128)S(1)}, f32[128,128]{1,0:T(8,128)S(1)}, u32[]{:S(2)}, u32[]{:S(2)}) collective-permute-start(f32[128,128]{1,0:T(8,128)S(1)} %get-tuple-element.61), channel_id=1, source_target_pairs={{0,1},{1,2},{2,3},{3,4},{4,5},{5,6},{6,7},{7,0},{8,9},{9,10},{10,1... | collective-permute-start | bytes 196616 | tf_op jit(solution)/shard_map/ppermute | solution.py:324
  68.8 6.1 %collective-permute-start.15 = (f32[128,128]{1,0:T(8,128)S(1)}, f32[128,128]{1,0:T(8,128)S(1)}, u32[]{:S(2)}, u32[]{:S(2)}) collective-permute-start(f32[128,128]{1,0:T(8,128)S(1)} %get-tuple-element.53), channel_id=1, source_target_pairs={{1,0},{2,1},{3,2},{4,3},{5,4},{6,5},{7,6},{0,7},{9,8},{10,9},{11,1... | collective-permute-start | bytes 196616 | tf_op jit(solution)/shard_map/ppermute | solution.py:324
  68.8 6.1 %collective-permute-start.14 = (f32[128,128]{1,0:T(8,128)S(1)}, f32[128,128]{1,0:T(8,128)S(1)}, u32[]{:S(2)}, u32[]{:S(2)}) collective-permute-start(f32[128,128]{1,0:T(8,128)S(1)} %get-tuple-element.53), channel_id=1, source_target_pairs={{0,1},{1,2},{2,3},{3,4},{4,5},{5,6},{6,7},{7,0},{8,9},{9,10},{10,1... | collective-permute-start | bytes 196616 | tf_op jit(solution)/shard_map/ppermute | solution.py:324
  (4 other events, 30.5 us)
